TPU v7x, 128 devices: a whole 4x4x4 slice. The times are simulated.
128 devices in a mesh: brick: 32 (over x, z, core), view: 4 (over y).
Axes of the slice: x: 4, y: 4, z: 4, core: 2. Of those that a mesh axis runs over, the one named last changes fastest.
Arguments:
- estimate: float32 [1024, 128, 128], P('brick'), may hold values from 0.5 to 2
- view_data: bfloat16 [8, 2048, 128, 128], P('view', 'brick'), may hold values from 0.25 to 4
- psf_taps: float32 [8, 3, 31], P('view'), may hold values from 0.05 to 1
- routes: int32 [8, 1024, 1], P('view'), may hold values from 0 to 31; in each aligned block of 32 rows (0 to 31, 32 to 63, ..., all dimensions but the last counted through in order) at most 2 rows name the same one
Outputs:
- merged: float32 [1024, 128, 128], P('brick')
Inputs may be any that keep to these rules, and one draw needn't show every extreme that they name: `routes`: in each view, among the 32 planes of one brick no owner is named more than 2 times, and some brick reaches 2.
All inputs are finite; a program needn't handle non-finite values.
Results may differ from a plain program's by a relative error of at most 0.0003.
Values may be sent and summed in bfloat16 or wider, within the bound.
No kernel may reach another device: no remote copies, remote signals or barrier semaphores. Data moves between devices by JAX's collectives and lax.ppermute only.
A program may use at most 128 MiB of HBM per device.

v0:
```python
from functools import partial

import jax
import jax.numpy as jnp
from jax import lax
from jax.experimental import pallas as pl
from jax.experimental.pallas import tpu as pltpu
from jax.sharding import PartitionSpec as P

VIEWS = 8
ITERS = 2
TAPS = 31
REACH = 16
BF16 = jnp.bfloat16
F32 = jnp.float32

BOTH = ("brick", "view")


def dot(a, b):
    return jnp.dot(a, b, preferred_element_type=F32)


def twice(a, axis):
    return jnp.concatenate([a, a], axis=axis)


def split(a):
    high = a.astype(BF16)
    return high, (a - high.astype(F32)).astype(BF16)


def blur_steps(fe, ax, ay, tz, t1, views, core, finish):
    ext_y = fe.shape[0]

    def along_x(step, carry):
        y0 = pl.multiple_of(step * 8, 8)
        rows = []
        for k in range(0, 8, 2):
            pair = jnp.concatenate([fe[y0 + k], fe[y0 + k + 1]], axis=1)
            out = dot(ax[...], twice(pair, 0))
            rows += [out[:, :128], out[:, 128:]]
        t1[:, pl.ds(y0, 8), :] = jnp.swapaxes(jnp.stack(rows), 0, 1)
        return carry

    lax.fori_loop(0, ext_y // 8, along_x, 0, unroll=True)

    def along_yz(v, carry):
        rows = []
        for i in range(0, core, 2):
            pair = jnp.concatenate([t1[v * core + i], t1[v * core + i + 1]], axis=1).astype(BF16)
            out = dot(ay[v], twice(pair, 0)).astype(BF16)
            rows += [out[:, :128], out[:, 128:]]
        plane = jnp.concatenate(rows, axis=0)
        finish(v, dot(twice(plane, 1), tz[v]))
        return carry

    lax.fori_loop(0, views, along_yz, 0, unroll=True)


def back_steps(ratio_of, axt, ayt, tzt, t1, out, views, core):
    def along_zy(v, carry):
        high, low = split(dot(twice(ratio_of(v), 1), tzt[v]))
        weights = twice(ayt[v], 1)
        for i in range(0, core, 2):
            here, there = slice(i * core, (i + 1) * core), slice((i + 1) * core, (i + 2) * core)
            pair = jnp.concatenate([high[here], high[there]], axis=1)
            rest = jnp.concatenate([low[here], low[there]], axis=1)
            rows = dot(weights, jnp.concatenate([pair, pair, rest, rest], axis=0))
            t1[v * core + i] = rows[:, :128]
            t1[v * core + i + 1] = rows[:, 128:]
        return carry

    lax.fori_loop(0, views, along_zy, 0, unroll=True)
    ext = out.shape[1]

    def along_x(step, carry):
        y0 = pl.multiple_of(step * 8, 8)
        high, low = split(jnp.swapaxes(t1[:, pl.ds(y0, 8), :], 0, 1))
        for k in range(0, 8, 2):
            both = dot(axt[...], jnp.concatenate([high[k], high[k + 1]], axis=1))
            rest = dot(axt[:ext], jnp.concatenate([low[k], low[k + 1]], axis=1))
            rows = both[:ext] + both[ext:] + rest
            out[y0 + k] = rows[:, :128]
            out[y0 + k + 1] = rows[:, 128:]
        return carry

    lax.fori_loop(0, out.shape[0] // 8, along_x, 0, unroll=True)


SHIFT = 256.0
LEVELS = 65534.0
HALF = 32767


def mark_of(part):
    top = jnp.max(jnp.max(part, axis=0), axis=0, keepdims=True)
    top = jnp.broadcast_to(jnp.max(top, axis=1, keepdims=True), (1, part.shape[-1]))
    return jnp.clip(jnp.ceil(jnp.log2(top)), -100.0, 120.0) + SHIFT


def encode(part, scale):
    return ((part * scale + 0.5).astype(jnp.int32) - HALF).astype(jnp.int16)


def decode(codes, scale):
    return (codes.astype(jnp.int32) + HALF).astype(F32) * scale


def scale_of(message):
    mark = message[message.shape[0] - 1, :16].astype(jnp.int32).astype(F32)[:1]
    return jnp.where(mark > 0, jnp.exp2(mark - SHIFT) / LEVELS, 0.0)


def in_blocks(count, body):
    def step(n, carry):
        body(pl.multiple_of(n * 8, 8))
        return carry

    lax.fori_loop(0, count // 8, step, 0)


def send_part(part, *messages):
    mark = mark_of(part[...])
    scale = jnp.exp2(SHIFT - mark) * LEVELS
    for out, y0, x0 in messages:
        count, width = out.shape[0] - 1, out.shape[1]

        def block(y):
            out[pl.ds(y, 8)] = encode(part[pl.ds(y0 + y, 8), x0 : x0 + width], scale)

        in_blocks(count, block)
        out[count] = jnp.broadcast_to(mark.astype(jnp.int32), out.shape[1:]).astype(jnp.int16)


def sides(odd, last):
    return (1 - odd) * last, odd * last


def odd_of(axis):
    return lax.rem(lax.axis_index(axis), 2)


def for_parity(odd, body):
    for value in (0, 1):
        pl.when(odd == value)(partial(body, value))


def prepare_kernel(estimate, middle, near, far):
    planes, size_y = estimate.shape[:2]
    count = middle.shape[0]
    first = lax.axis_index("view") * (count - 2 * REACH) - REACH
    for y in range(0, count, 8):
        at = first + y
        inside = jnp.logical_and(at >= 0, at < size_y)
        rows = estimate[:, pl.ds(pl.multiple_of(jnp.clip(at, 0, size_y - 8), 8), 8), :]
        middle[y : y + 8] = jnp.where(inside, jnp.swapaxes(rows, 0, 1), 0.0)

    def send(odd):
        x_near, x_far = sides(odd, planes - REACH)
        near[...] = middle[:, x_near : x_near + REACH].astype(BF16)
        far[...] = middle[:, x_far : x_far + REACH].astype(BF16)

    for_parity(odd_of("brick"), send)


def deal_kernel(data, out, stage, sems):
    views, groups, core = data.shape[0], out.shape[1], out.shape[4]
    parts = [(v, q) for v in range(views) for q in range(groups)]
    loads, stores = [], []
    for n, (v, q) in enumerate(parts):
        rows = data.at[v, :, :, q * core : (q + 1) * core, :]
        loads.append(pltpu.make_async_copy(rows, stage.at[n], sems.at[0, n]))
        stores.append(pltpu.make_async_copy(stage.at[n], out.at[:, q, v], sems.at[1, n]))
    for load in loads:
        load.start()
    for load, store in zip(loads, stores):
        load.wait()
        store.start()
    for store in stores:
        store.wait()


def blur_kernel(near, middle, far, ax, ay, tz, out, fe, t1):
    views, core = ay.shape[0], ay.shape[1]

    def join(odd):
        x_near, x_far = sides(odd, REACH + core)
        fe[:, x_near : x_near + REACH] = near[...]
        fe[:, REACH : REACH + core] = middle[...].astype(BF16)
        fe[:, x_far : x_far + REACH] = far[...]

    for_parity(odd_of("brick"), join)

    def finish(v, rows):
        out[v] = rows.astype(BF16)

    blur_steps(fe, ax, ay, tz, t1, views, core, finish)


def ratio_rows(v, core, where, got, den):
    rows = [got[where[v * core + x]] for x in range(core)]
    data = jnp.concatenate(rows, axis=0).astype(F32)
    return (data / den.astype(F32)).astype(BF16)


def back_kernel(where, blurred, got, axt, ayt, tzt, out, nn, fn, nf, ff, t1):
    views, core = ayt.shape[0], got.shape[1]
    back_steps(
        lambda v: ratio_rows(v, core, where, got, blurred[v]), axt, ayt, tzt, t1, out, views, core
    )
    y_near, y_far = sides(odd_of("view"), out.shape[0] // 2)

    def send(odd):
        x_near, x_far = sides(odd, out.shape[1] - nn.shape[1])
        send_part(
            out, (nn, y_near, x_near), (fn, y_near, x_far), (nf, y_far, x_near), (ff, y_far, x_far)
        )

    for_parity(odd_of("brick"), send)


def full_kernel(
    where, near, middle, far, total_near, total_far, got_near, got_far,
    got, ax, ay, tz, axt, ayt, tzt, kept, out, send_near, send_far, fe, t1, ratios,
):
    views, core = ay.shape[0], ay.shape[1]
    y_near, y_far = sides(odd_of("view"), out.shape[0] // 2)

    def renew(odd):
        x_near, x_far = sides(odd, REACH + core)
        fields = (near, x_near, REACH), (far, x_far, REACH), (middle, REACH, core)
        for codes, total, first in ((got_near, total_near, y_near), (got_far, total_far, y_far)):
            scale = scale_of(codes)

            def block(y):
                rows, here = pl.ds(first + y, 8), pl.ds(y, 8)
                for field, x, width in fields:
                    cells = slice(x, x + width)
                    step = (total[here, cells] + decode(codes[here, cells], scale)) / views
                    fresh = field[rows].astype(F32) * step
                    fe[rows, cells] = fresh.astype(BF16)
                    if field is middle:
                        kept[rows] = fresh

            in_blocks(total.shape[0], block)

    for_parity(odd_of("brick"), renew)

    def finish(v, rows):
        ratios[v] = ratio_rows(v, core, where, got, rows.astype(BF16))

    blur_steps(fe, ax, ay, tz, t1, views, core, finish)
    back_steps(lambda v: ratios[v], axt, ayt, tzt, t1, out, views, core)

    def send(odd):
        x_near, x_far = sides(odd, out.shape[1] - REACH)
        send_part(out, (send_near, 0, x_near), (send_far, 0, x_far))

    for_parity(odd_of("brick"), send)


def gather_rows(first, part, near, far, out):
    side = near.shape[1]
    off = (part.shape[1] - 2 * side) // 2
    scale_n, scale_f = scale_of(near), scale_of(far)

    def add_both(odd):
        x_near, x_far = sides(odd, side)

        def block(y):
            rows = pl.ds(y, 8)
            for got, scale, x in ((near, scale_n, x_near), (far, scale_f, x_far)):
                here = part[pl.ds(first + y, 8), off + x : off + x + side]
                out[rows, x : x + side] = here + decode(got[rows], scale)

        in_blocks(out.shape[0], block)

    for_parity(odd_of("brick"), add_both)


def gather_half_kernel(which, part, near, far, out, message):
    first = sides(odd_of("view"), part.shape[0] // 2)[which]
    gather_rows(first, part, near, far, out)
    send_part(out, (message, 0, 0))


def gather_all_kernel(part, near, far, out, send_near, send_far):
    gather_rows(0, part, near, far, out)
    y_near, y_far = sides(odd_of("view"), part.shape[0] - REACH)
    send_part(out, (send_near, y_near, 0), (send_far, y_far, 0))


def last_kernel(field, total, near, far, codes_lo, codes_hi, fresh):
    y_near, y_far = sides(odd_of("view"), REACH)
    for got, first in ((near, y_near), (far, y_far)):
        scale = scale_of(got)

        def block(y):
            rows = pl.ds(REACH + first + y, 8)
            step = (total[rows] + decode(got[pl.ds(y, 8)], scale)) / VIEWS
            fresh[pl.ds(first + y, 8)] = field[rows] * step

        in_blocks(REACH, block)
    send_part(fresh, (codes_lo, 0, 0), (codes_hi, fresh.shape[0] // 2, 0))


def place_rows(message, write):
    scale = scale_of(message)
    for y in range(0, message.shape[0] - 1, 8):
        write(y, jnp.swapaxes(decode(message[y : y + 8], scale), 0, 1))


def groups_around(group, count):
    far = lax.rem(group + 2 * lax.rem(group, 2) - 1 + count, count)
    return group, group + 1 - 2 * lax.rem(group, 2), far, lax.rem(group + 2, count)


def place_kernel(groups, *refs):
    order = groups_around(lax.axis_index("view"), groups)
    out = refs[-1]
    half = refs[0].shape[0] - 1
    for n, message in enumerate(refs[:-1]):

        def write(y, rows):
            at = pl.multiple_of((2 * order[n // 2] + n % 2) * half + y, 8)
            out[:, pl.ds(at, 8), :] = rows

        place_rows(message, write)


def finish_kernel(groups, lower, upper, _, out, rows, sem):
    order = groups_around(lax.axis_index("view"), groups)
    half = lower.shape[0] - 1
    copies = []
    for n, message in enumerate((lower, upper)):

        def write(y, block):
            rows[:, n * half + y : n * half + y + 8, :] = block

        place_rows(message, write)
        at = pl.multiple_of((order[3] * 2 + n) * half, 8)
        part = rows.at[:, n * half : (n + 1) * half, :]
        copies.append(pltpu.make_async_copy(part, out.at[:, pl.ds(at, half), :], sem.at[n]))
        copies[n].start()
    for copy in copies:
        copy.wait()


VMEM = pl.BlockSpec(memory_space=pltpu.VMEM)
SMEM = pl.BlockSpec(memory_space=pltpu.SMEM)
ANY = pl.BlockSpec(memory_space=pl.ANY)


def call(kernel, out_shape, scratch, flops, *operands, scalars=0, space=VMEM, limit=36 << 20):
    size = sum(a.size * a.dtype.itemsize for a in operands)
    return pl.pallas_call(
        kernel,
        out_shape=out_shape,
        in_specs=[SMEM] * scalars + [space] * (len(operands) - scalars),
        out_specs=jax.tree.map(lambda _: space, out_shape),
        scratch_shapes=scratch,
        compiler_params=pltpu.CompilerParams(vmem_limit_bytes=limit),
        cost_estimate=pl.CostEstimate(flops=flops, bytes_accessed=size, transcendentals=0),
    )(*operands)


def halves(a, axis):
    high = lax.reduce_precision(a, 8, 7)
    return jnp.concatenate([high, a - high], axis=axis).astype(BF16)


def banded(taps, rows, cols, shift):
    offset = jnp.arange(rows)[:, None] - jnp.arange(cols)[None, :] + shift
    select = (offset[None] == jnp.arange(TAPS)[:, None, None]).astype(F32)
    return jnp.einsum("vt,trc->vrc", taps, select, precision=lax.Precision.HIGHEST)


def swap_near(a, axis):
    return lax.ppermute(a, axis, [(i, i ^ 1) for i in range(lax.axis_size(axis))])


def swap_far(a, axis, ring=False):
    count = lax.axis_size(axis)
    pairs = [(i, i + 1) for i in range(1, count - 1, 2)] + ([(count - 1, 0)] if ring else [])
    return lax.ppermute(a, axis, pairs + [(j, i) for i, j in pairs])


def per_device(estimate, view_data, psf_taps, routes):
    bricks, groups = lax.axis_size("brick"), lax.axis_size("view")
    brick, group = lax.axis_index("brick"), lax.axis_index("view")
    planes, size_y, size_z = estimate.shape
    views_dev, slots = view_data.shape[:2]
    capacity = slots // bricks
    core = size_y // groups
    ext = core + 2 * REACH
    views = views_dev * groups

    def shape(*dims, kind=F32):
        return jax.ShapeDtypeStruct(dims + (size_z,), kind)

    middle, near, far = call(
        prepare_kernel,
        (shape(ext, planes), shape(ext, REACH, kind=BF16), shape(ext, REACH, kind=BF16)),
        [],
        0,
        estimate,
    )
    near, far, psf_taps, routes = lax.optimization_barrier((near, far, psf_taps, routes))
    near, far = swap_near(near, "brick"), swap_far(far, "brick")

    normed = psf_taps / jnp.sum(psf_taps, axis=-1, keepdims=True)
    blocks = routes[..., 0].reshape(views_dev, bricks, planes)
    own = lax.dynamic_index_in_dim(blocks, brick, 1, keepdims=False)
    position = jnp.arange(planes)
    earlier = position[:, None] < position[None, :]
    rank = jnp.sum(((own[:, :, None] == own[:, None, :]) & earlier).astype(jnp.int32), axis=1)
    view_id = jnp.arange(views_dev)[:, None]
    where = ((own * groups + group) * views_dev + view_id) * capacity + rank
    packed = jnp.concatenate(
        [normed.reshape(views_dev, 3 * TAPS), where.astype(F32)], axis=1
    )
    packed = jnp.pad(packed, ((0, 0), (0, 128 - packed.shape[1])))
    across = lax.ppermute(packed, "view", [(i, (i + 2) % groups) for i in range(groups)])
    around = [packed, swap_near(packed, "view"), swap_far(packed, "view", True), across]
    order = jnp.stack([group, group ^ 1, (group + 2 * (group % 2) - 1) % groups, (group + 2) % groups])
    here = order[:, None] == jnp.arange(groups)[None, :]
    packed = jnp.sum(jnp.where(here[:, :, None, None], jnp.stack(around)[:, None], 0.0), axis=0)
    packed = packed.reshape(views, packed.shape[-1])

    sending = call(
        deal_kernel,
        shape(bricks, groups, views_dev, capacity, core, kind=BF16),
        [
            pltpu.VMEM((views_dev * groups, bricks, capacity, core, size_z), BF16),
            pltpu.SemaphoreType.DMA((2, views_dev * groups)),
        ],
        0,
        view_data.reshape(views_dev, bricks, capacity, size_y, size_z),
        space=ANY,
        limit=58 << 20,
    )
    sending = sending.reshape(bricks * groups, views_dev * capacity, core, size_z)
    sending, near, far, packed = lax.optimization_barrier((sending, near, far, packed))
    got = lax.all_to_all(sending, BOTH, 0, 0, tiled=True)
    got = got.reshape(bricks * groups * views_dev * capacity, core, size_z)

    taps = packed[:, : 3 * TAPS].reshape(views, 3, TAPS)
    where = packed[:, 3 * TAPS : 3 * TAPS + planes].astype(jnp.int32).reshape(views * planes)

    mat_x = banded(taps[:, 0], ext, planes, -1)
    mat_y = banded(taps[:, 1], ext, core, -1)
    mat_z = banded(taps[:, 2], size_z, size_z, TAPS // 2)
    ax = halves(mat_x.transpose(0, 2, 1).reshape(views * planes, ext), 1)
    ay = halves(mat_y.transpose(0, 2, 1), 2)
    tz = halves(mat_z, 1)
    axt = halves(mat_x.transpose(1, 0, 2).reshape(ext, views * planes), 0)
    ayt = halves(mat_y, 2)
    tzt = halves(mat_z.transpose(0, 2, 1), 1)

    scratch = pltpu.VMEM((views * planes, ext, size_z), F32)
    wide = pltpu.VMEM((ext, ext, size_z), BF16)
    codes = partial(shape, kind=jnp.int16)
    flops = 4 * 10**9
    rows_shape = (views, planes * core, size_z)
    forward, back = (ax, ay, tz), (axt, ayt, tzt)
    field = (near, middle, far)

    blurred = call(
        blur_kernel,
        jax.ShapeDtypeStruct(rows_shape, BF16),
        [wide, scratch],
        flops,
        *field,
        *forward,
    )
    side = 2 * REACH
    part, nn, fn, nf, ff = call(
        back_kernel,
        (shape(ext, ext),) + (codes(side + 1, side),) * 4,
        [scratch],
        flops,
        where,
        blurred,
        got,
        *back,
        scalars=1,
    )
    parts = swap_near(nn, "brick"), swap_far(fn, "brick")
    others = swap_near(nf, "brick"), swap_far(ff, "brick")
    half_shape = (shape(side, ext), codes(side + 1, ext))
    total_near, send_near = call(
        partial(gather_half_kernel, 0), half_shape, [], 0, part, *parts
    )
    total_far, send_far = call(
        partial(gather_half_kernel, 1), half_shape, [], 0, part, *others
    )
    side = REACH
    kept, part, send_near, send_far = call(
        full_kernel,
        (shape(ext, planes), shape(ext, ext), codes(ext + 1, side), codes(ext + 1, side)),
        [wide, scratch, pltpu.VMEM(rows_shape, BF16)],
        2 * flops,
        where,
        *field,
        total_near,
        total_far,
        swap_near(send_near, "view"),
        swap_far(send_far, "view"),
        got,
        *forward,
        *back,
        scalars=1,
    )
    total, send_near, send_far = call(
        gather_all_kernel,
        (shape(ext, planes), codes(side + 1, planes), codes(side + 1, planes)),
        [],
        0,
        part,
        swap_near(send_near, "brick"),
        swap_far(send_far, "brick"),
    )
    lower, upper = call(
        last_kernel,
        (codes(core // 2 + 1, planes),) * 2,
        [pltpu.VMEM((core, planes, size_z), F32)],
        0,
        kept,
        total,
        swap_near(send_near, "view"),
        swap_far(send_far, "view"),
    )
    lower_far, upper_near = swap_far(lower, "view", True), swap_near(upper, "view")
    upper_far, lower_near = swap_far(upper, "view", True), swap_near(lower, "view")
    lower_last, upper_last = swap_near(lower_far, "view"), swap_far(upper_near, "view", True)
    merged = call(
        partial(place_kernel, groups),
        shape(planes, size_y),
        [],
        0,
        lower,
        upper,
        lower_near,
        upper_near,
        lower_far,
        upper_far,
    )
    return pl.pallas_call(
        partial(finish_kernel, groups),
        out_shape=shape(planes, size_y),
        in_specs=[VMEM, VMEM, ANY],
        out_specs=ANY,
        scratch_shapes=[pltpu.VMEM((planes, core, size_z), F32), pltpu.SemaphoreType.DMA((2,))],
        input_output_aliases={2: 0},
        compiler_params=pltpu.CompilerParams(vmem_limit_bytes=36 << 20),
    )(lower_last, upper_last, merged)


def solution(mesh):
    return jax.shard_map(
        per_device,
        mesh=mesh,
        in_specs=(
            P("brick", None, None),
            P("view", "brick", None, None),
            P("view", None, None),
            P("view", None, None),
        ),
        out_specs=P("brick", None, None),
        check_vma=False,
    )
```

profile of v0, /device:TPU:2, one launch (start us, length us, event | category | flops | bytes accessed | tf_op | source)
XLA Modules:
  0.0 162.2 jit_solution(8779298887200902054)
XLA Ops:
  0.0 1.6 copy-done
  2.5 3.0 %collective-permute-start.3 = (f32[2,128]{1,0:T(2,128)S(1)}, f32[2,128]{1,0:T(2,128)S(1)}, u32[]{:S(2)}, u32[]{:S(2)}) collective-permute-start(f32[2,128]{1,0:T(2,128)S(1)} %select_maximum_fusion), channel_id=1, source_target_pairs={{1,2},{3,0},{2,1},{0,3},{5,6},{7,4},{6,5},{4,7},{9,10},{11,8},{10,... | collective-permute-start | bytes 3080 | tf_op jit(solution)/shard_map/ppermute | solution.py:386
  5.7 1.5 collective-permute-start.4
  7.2 6.0 %collective-permute-start.1 = (bf16[64,16,128]{2,1,0:T(8,128)(2,1)S(1)}, bf16[64,16,128]{2,1,0:T(8,128)(2,1)S(1)}, u32[]{:S(2)}, u32[]{:S(2)}) collective-permute-start(bf16[64,16,128]{2,1,0:T(8,128)(2,1)S(1)} %get-tuple-element.37), channel_id=1, source_target_pairs={{4,8},{12,16},{20,24},{28,32},{36,40},{44,48},{52,56},{60,64},{68,... | collective-permute-start | bytes 786440 | tf_op jit(solution)/shard_map/ppermute | solution.py:386
  13.4 3.8 %shard_map.46 = bf16[32,4,2,2,32,128]{5,4,3,2,1,0:T(8,128)(2,1)} custom-call(bf16[2,32,2,128,128]{4,3,2,1,0:T(8,128)(2,1)} %bitcast.44), custom_call_target="tpu_custom_call" | custom-call | bytes 4194304 | tf_op jit(solution)/shard_map/pallas_call | solution.py:357
  17.4 10.6 %all-to-all-start = ((bf16[128,4,32,128]{3,2,1,0:T(8,128)(2,1)}), bf16[128,4,32,128]{3,2,1,0:T(8,128)(2,1)}, u32[]{:S(2)}, u32[]{:S(2)}) async-start(bf16[128,4,32,128]{3,2,1,0:T(8,128)(2,1)} %bitcast.43), calls=%async_computation | async-start | bytes 8388608 | tf_op jit(solution)/shard_map/all_to_all | solution.py:445
  32.6 4.5 %shard_map.48.blurred = bf16[8,1024,128]{2,1,0:T(8,128)(2,1)S(1)} custom-call(bf16[64,16,128]{2,1,0:T(8,128)(2,1)S(1)} %collective-permute-done.near, f32[64,32,128]{2,1,0:T(8,128)S(1)} %get-tuple-element.42.middle, bf16[64,16,128]{2,1,0:T(8,128)(2,1)S(1)} %collective-permute-done.1.far, bf16[256,128]{1,0:T(8,128)(2,1)S(1)} %pad_maximum_fusion.3.ax, ...), custom_call_target="tpu_custom_call" | custom-call | flops 4000000000 | bytes 2228224 | tf_op jit(solution)/shard_map/pallas_call | solution.py:357
  38.5 41.4 %all-to-all-done = bf16[128,4,32,128]{3,2,1,0:T(8,128)(2,1)} async-done(((bf16[128,4,32,128]{3,2,1,0:T(8,128)(2,1)}), bf16[128,4,32,128]{3,2,1,0:T(8,128)(2,1)}, u32[]{:S(2)}, u32[]{:S(2)}) %all-to-all-start) | async-done | bytes 4194336 | tf_op jit(solution)/shard_map/all_to_all | solution.py:445
  79.9 1.6 copy-done.2
  81.5 7.9 %shard_map.49 = (f32[64,64,128]{2,1,0:T(8,128)S(1)}, s16[33,32,128]{2,1,0:T(8,128)(2,1)S(1)}, s16[33,32,128]{2,1,0:T(8,128)(2,1)S(1)}, s16[33,32,128]{2,1,0:T(8,128)(2,1)S(1)}, s16[33,32,128]{2,1,0:T(8,128)(2,1)S(1)}) custom-call(s32[256]{0:T(256)S(1)} %reshape.94.where, bf16[8,1024,128]{2,1,0:T(8,128)(2,1)S(1)} %copy-done.2, ...), custom_call_target="tpu_custom_call" | custom-call | flops 4000000000 | bytes 6947840 | tf_op jit(solution)/shard_map/pallas_call | solution.py:357
  89.8 2.9 %collective-permute-start.8 = (s16[33,32,128]{2,1,0:T(8,128)(2,1)S(1)}, s16[33,32,128]{2,1,0:T(8,128)(2,1)S(1)}, u32[]{:S(2)}, u32[]{:S(2)}) collective-permute-start(s16[33,32,128]{2,1,0:T(8,128)(2,1)S(1)} %get-tuple-element.50), channel_id=1, source_target_pairs={{4,8},{12,16},{20,24},{28,32},{36,40},{44,48},{52,56},{60,64},{68,... | collective-permute-start | bytes 811016 | tf_op jit(solution)/shard_map/ppermute | solution.py:386
  92.9 4.7 %collective-permute-start.6 = (s16[33,32,128]{2,1,0:T(8,128)(2,1)S(1)}, s16[33,32,128]{2,1,0:T(8,128)(2,1)S(1)}, u32[]{:S(2)}, u32[]{:S(2)}) collective-permute-start(s16[33,32,128]{2,1,0:T(8,128)(2,1)S(1)} %get-tuple-element.47), channel_id=1, source_target_pairs={{4,8},{12,16},{20,24},{28,32},{36,40},{44,48},{52,56},{60,64},{68,... | collective-permute-start | bytes 811016 | tf_op jit(solution)/shard_map/ppermute | solution.py:386
  97.6 2.1 %collective-permute-done.8.far = s16[33,32,128]{2,1,0:T(8,128)(2,1)S(1)} collective-permute-done((s16[33,32,128]{2,1,0:T(8,128)(2,1)S(1)}, s16[33,32,128]{2,1,0:T(8,128)(2,1)S(1)}, u32[]{:S(2)}, u32[]{:S(2)}) %collective-permute-start.8) | collective-permute-done | bytes 270368 | tf_op jit(solution)/shard_map/ppermute | solution.py:386
  101.2 1.6 collective-permute-done.6.far
  104.5 11.9 %collective-permute-done.9.got_near = s16[33,64,128]{2,1,0:T(8,128)(2,1)S(1)} collective-permute-done((s16[33,64,128]{2,1,0:T(8,128)(2,1)S(1)}, s16[33,64,128]{2,1,0:T(8,128)(2,1)S(1)}, u32[]{:S(2)}, u32[]{:S(2)}) %collective-permute-start.9) | collective-permute-done | bytes 540704 | tf_op jit(solution)/shard_map/ppermute | solution.py:380
  116.4 12.3 %shard_map.52 = (f32[64,32,128]{2,1,0:T(8,128)S(1)}, f32[64,64,128]{2,1,0:T(8,128)S(1)}, s16[65,16,128]{2,1,0:T(8,128)(2,1)S(1)}, s16[65,16,128]{2,1,0:T(8,128)(2,1)S(1)}) custom-call(s32[256]{0:T(256)S(1)} %reshape.94.where, bf16[64,16,128]{2,1,0:T(8,128)(2,1)S(1)} %collective-permute-done.near, f32[64,32,128]{2,1,0:T(8,128)S(1)} %get-tuple-element.42.middle, ...), custom_call_target="tpu_custom_call" | custom-call | flops 8000000000 | bytes 10257408 | tf_op jit(solution)/shard_map/pallas_call | solution.py:357
  128.8 4.8 %collective-permute-start.12 = (s16[65,16,128]{2,1,0:T(8,128)(2,1)S(1)}, s16[65,16,128]{2,1,0:T(8,128)(2,1)S(1)}, u32[]{:S(2)}, u32[]{:S(2)}) collective-permute-start(s16[65,16,128]{2,1,0:T(8,128)(2,1)S(1)} %get-tuple-element.57), channel_id=1, source_target_pairs={{4,8},{12,16},{20,24},{28,32},{36,40},{44,48},{52,56},{60,64},{68,... | collective-permute-start | bytes 798728 | tf_op jit(solution)/shard_map/ppermute | solution.py:386
  133.6 5.1 %collective-permute-done.12.far = s16[65,16,128]{2,1,0:T(8,128)(2,1)S(1)} collective-permute-done((s16[65,16,128]{2,1,0:T(8,128)(2,1)S(1)}, s16[65,16,128]{2,1,0:T(8,128)(2,1)S(1)}, u32[]{:S(2)}, u32[]{:S(2)}) %collective-permute-start.12) | collective-permute-done | bytes 266272 | tf_op jit(solution)/shard_map/ppermute | solution.py:386
  140.8 3.7 %collective-permute-done.13.near = s16[17,32,128]{2,1,0:T(8,128)(2,1)S(1)} collective-permute-done((s16[17,32,128]{2,1,0:T(8,128)(2,1)S(1)}, s16[17,32,128]{2,1,0:T(8,128)(2,1)S(1)}, u32[]{:S(2)}, u32[]{:S(2)}) %collective-permute-start.13) | collective-permute-done | bytes 139296 | tf_op jit(solution)/shard_map/ppermute | solution.py:380
  146.5 3.3 %collective-permute-start.17 = (s16[17,32,128]{2,1,0:T(8,128)(2,1)S(1)}, s16[17,32,128]{2,1,0:T(8,128)(2,1)S(1)}, u32[]{:S(2)}, u32[]{:S(2)}) collective-permute-start(s16[17,32,128]{2,1,0:T(8,128)(2,1)S(1)} %get-tuple-element.62.refs_1_), channel_id=1, source_target_pairs={{0,1},{1,0},{2,3},{3,2},{4,5},{5,4},{6,7},{7,6},{8,9},{9,8},{10,11... | collective-permute-start | bytes 417800 | tf_op jit(solution)/shard_map/ppermute | solution.py:380
  149.8 1.8 %collective-permute-start.20 = (s16[17,32,128]{2,1,0:T(8,128)(2,1)S(1)}, s16[17,32,128]{2,1,0:T(8,128)(2,1)S(1)}, u32[]{:S(2)}, u32[]{:S(2)}) collective-permute-start(s16[17,32,128]{2,1,0:T(8,128)(2,1)S(1)} %get-tuple-element.62.refs_1_), channel_id=1, source_target_pairs={{1,2},{3,0},{2,1},{0,3},{5,6},{7,4},{6,5},{4,7},{9,10},{11,8},{10,... | collective-permute-start | bytes 417800 | tf_op jit(solution)/shard_map/ppermute | solution.py:386
  152.4 2.4 %collective-permute-start.16 = (s16[17,32,128]{2,1,0:T(8,128)(2,1)S(1)}, s16[17,32,128]{2,1,0:T(8,128)(2,1)S(1)}, u32[]{:S(2)}, u32[]{:S(2)}) collective-permute-start(s16[17,32,128]{2,1,0:T(8,128)(2,1)S(1)} %collective-permute-done.15.refs_4_), channel_id=1, source_target_pairs={{0,1},{1,0},{2,3},{3,2},{4,5},{5,4},{6,7},{7,6},{8,9},{9,8},{10,11... | collective-permute-start | bytes 417800 | tf_op jit(solution)/shard_map/ppermute | solution.py:380
  156.6 1.8 %shard_map.55._ = f32[32,128,128]{2,1,0:T(8,128)} custom-call(s16[17,32,128]{2,1,0:T(8,128)(2,1)S(1)} %get-tuple-element.61.refs_0_, s16[17,32,128]{2,1,0:T(8,128)(2,1)S(1)} %get-tuple-element.62.refs_1_, s16[17,32,128]{2,1,0:T(8,128)(2,1)S(1)} %collective-permute-done.19.refs_2_, s16[17,32,128]{2,1,0:T(8,128)(2,1)S(1)} %collective-permute-done.17.refs_3_, ...), custom_call_target="tpu_custom_call" | custom-call | bytes 835584 | tf_op jit(solution)/shard_map/pallas_call | solution.py:357
  158.4 2.7 %collective-permute-done.18.upper = s16[17,32,128]{2,1,0:T(8,128)(2,1)S(1)} collective-permute-done((s16[17,32,128]{2,1,0:T(8,128)(2,1)S(1)}, s16[17,32,128]{2,1,0:T(8,128)(2,1)S(1)}, u32[]{:S(2)}, u32[]{:S(2)}) %collective-permute-start.18) | collective-permute-done | bytes 139296 | tf_op jit(solution)/shard_map/ppermute | solution.py:386
  (84 shorter events, 18.5 us)
Async XLA Ops:
  0.0 2.2 %copy-start.4 = (s32[2,1024,1]{1,2,0:T(1,128)S(1)}, s32[2,1024,1]{1,2,0:T(1,128)}, u32[]{:S(2)}) copy-start(s32[2,1024,1]{1,2,0:T(1,128)} %param.7) | copy-start | bytes 24580
  0.0 1.9 %copy-start.3 = (f32[2,3,31]{2,0,1:T(2,128)S(1)}, f32[2,3,31]{2,0,1:T(2,128)}, u32[]{:S(2)}) copy-start(f32[2,3,31]{2,0,1:T(2,128)} %param.6) | copy-start | bytes 2236
  2.5 14.7 %collective-permute-start.3 = (f32[2,128]{1,0:T(2,128)S(1)}, f32[2,128]{1,0:T(2,128)S(1)}, u32[]{:S(2)}, u32[]{:S(2)}) collective-permute-start(f32[2,128]{1,0:T(2,128)S(1)} %select_maximum_fusion), channel_id=1, source_target_pairs={{1,2},{3,0},{2,1},{0,3},{5,6},{7,4},{6,5},{4,7},{9,10},{11,8},{10,... | collective-permute-start | bytes 3080 | tf_op jit(solution)/shard_map/ppermute | solution.py:386
  5.5 11.7 %collective-permute-start.2 = (f32[2,128]{1,0:T(2,128)S(1)}, f32[2,128]{1,0:T(2,128)S(1)}, u32[]{:S(2)}, u32[]{:S(2)}) collective-permute-start(f32[2,128]{1,0:T(2,128)S(1)} %select_maximum_fusion), channel_id=1, source_target_pairs={{0,1},{1,0},{2,3},{3,2},{4,5},{5,4},{6,7},{7,6},{8,9},{9,8},{10,11... | collective-permute-start | bytes 3080 | tf_op jit(solution)/shard_map/ppermute | solution.py:380
  5.7 11.6 %collective-permute-start.4 = (f32[2,128]{1,0:T(2,128)S(1)}, f32[2,128]{1,0:T(2,128)S(1)}, u32[]{:S(2)}, u32[]{:S(2)}) collective-permute-start(f32[2,128]{1,0:T(2,128)S(1)} %select_maximum_fusion), channel_id=1, source_target_pairs={{0,2},{1,3},{2,0},{3,1},{4,6},{5,7},{6,4},{7,5},{8,10},{9,11},{10,... | collective-permute-start | bytes 3080 | tf_op jit(solution)/shard_map/ppermute | solution.py:424
  7.2 10.1 %collective-permute-start = (bf16[64,16,128]{2,1,0:T(8,128)(2,1)S(1)}, bf16[64,16,128]{2,1,0:T(8,128)(2,1)S(1)}, u32[]{:S(2)}, u32[]{:S(2)}) collective-permute-start(bf16[64,16,128]{2,1,0:T(8,128)(2,1)S(1)} %get-tuple-element.36), channel_id=1, source_target_pairs={{0,4},{4,0},{8,12},{12,8},{16,20},{20,16},{24,28},{28,24},{32,36},... | collective-permute-start | bytes 786440 | tf_op jit(solution)/shard_map/ppermute | solution.py:380
  7.2 10.1 %collective-permute-start.1 = (bf16[64,16,128]{2,1,0:T(8,128)(2,1)S(1)}, bf16[64,16,128]{2,1,0:T(8,128)(2,1)S(1)}, u32[]{:S(2)}, u32[]{:S(2)}) collective-permute-start(bf16[64,16,128]{2,1,0:T(8,128)(2,1)S(1)} %get-tuple-element.37), channel_id=1, source_target_pairs={{4,8},{12,16},{20,24},{28,32},{36,40},{44,48},{52,56},{60,64},{68,... | collective-permute-start | bytes 786440 | tf_op jit(solution)/shard_map/ppermute | solution.py:386
  17.4 62.5 %all-to-all-start = ((bf16[128,4,32,128]{3,2,1,0:T(8,128)(2,1)}), bf16[128,4,32,128]{3,2,1,0:T(8,128)(2,1)}, u32[]{:S(2)}, u32[]{:S(2)}) async-start(bf16[128,4,32,128]{3,2,1,0:T(8,128)(2,1)} %bitcast.43), calls=%async_computation | async-start | bytes 8388608 | tf_op jit(solution)/shard_map/all_to_all | solution.py:445
  89.4 8.2 %collective-permute-start.7 = (s16[33,32,128]{2,1,0:T(8,128)(2,1)S(1)}, s16[33,32,128]{2,1,0:T(8,128)(2,1)S(1)}, u32[]{:S(2)}, u32[]{:S(2)}) collective-permute-start(s16[33,32,128]{2,1,0:T(8,128)(2,1)S(1)} %get-tuple-element.49), channel_id=1, source_target_pairs={{0,4},{4,0},{8,12},{12,8},{16,20},{20,16},{24,28},{28,24},{32,36},... | collective-permute-start | bytes 811016 | tf_op jit(solution)/shard_map/ppermute | solution.py:380
  89.8 9.9 %collective-permute-start.8 = (s16[33,32,128]{2,1,0:T(8,128)(2,1)S(1)}, s16[33,32,128]{2,1,0:T(8,128)(2,1)S(1)}, u32[]{:S(2)}, u32[]{:S(2)}) collective-permute-start(s16[33,32,128]{2,1,0:T(8,128)(2,1)S(1)} %get-tuple-element.50), channel_id=1, source_target_pairs={{4,8},{12,16},{20,24},{28,32},{36,40},{44,48},{52,56},{60,64},{68,... | collective-permute-start | bytes 811016 | tf_op jit(solution)/shard_map/ppermute | solution.py:386
  92.8 8.4 %collective-permute-start.5 = (s16[33,32,128]{2,1,0:T(8,128)(2,1)S(1)}, s16[33,32,128]{2,1,0:T(8,128)(2,1)S(1)}, u32[]{:S(2)}, u32[]{:S(2)}) collective-permute-start(s16[33,32,128]{2,1,0:T(8,128)(2,1)S(1)} %get-tuple-element.46), channel_id=1, source_target_pairs={{0,4},{4,0},{8,12},{12,8},{16,20},{20,16},{24,28},{28,24},{32,36},... | collective-permute-start | bytes 811016 | tf_op jit(solution)/shard_map/ppermute | solution.py:380
  92.9 9.9 %collective-permute-start.6 = (s16[33,32,128]{2,1,0:T(8,128)(2,1)S(1)}, s16[33,32,128]{2,1,0:T(8,128)(2,1)S(1)}, u32[]{:S(2)}, u32[]{:S(2)}) collective-permute-start(s16[33,32,128]{2,1,0:T(8,128)(2,1)S(1)} %get-tuple-element.47), channel_id=1, source_target_pairs={{4,8},{12,16},{20,24},{28,32},{36,40},{44,48},{52,56},{60,64},{68,... | collective-permute-start | bytes 811016 | tf_op jit(solution)/shard_map/ppermute | solution.py:386
  100.5 4.1 %collective-permute-start.10 = (s16[33,64,128]{2,1,0:T(8,128)(2,1)S(1)}, s16[33,64,128]{2,1,0:T(8,128)(2,1)S(1)}, u32[]{:S(2)}, u32[]{:S(2)}) collective-permute-start(s16[33,64,128]{2,1,0:T(8,128)(2,1)S(1)} %get-tuple-element.53), channel_id=1, source_target_pairs={{1,2},{2,1},{5,6},{6,5},{9,10},{10,9},{13,14},{14,13},{17,18},{18,... | collective-permute-start | bytes 1622024 | tf_op jit(solution)/shard_map/ppermute | solution.py:386
  103.5 12.9 %collective-permute-start.9 = (s16[33,64,128]{2,1,0:T(8,128)(2,1)S(1)}, s16[33,64,128]{2,1,0:T(8,128)(2,1)S(1)}, u32[]{:S(2)}, u32[]{:S(2)}) collective-permute-start(s16[33,64,128]{2,1,0:T(8,128)(2,1)S(1)} %get-tuple-element.52), channel_id=1, source_target_pairs={{0,1},{1,0},{2,3},{3,2},{4,5},{5,4},{6,7},{7,6},{8,9},{9,8},{10,11... | collective-permute-start | bytes 1622024 | tf_op jit(solution)/shard_map/ppermute | solution.py:380
  128.7 4.9 %collective-permute-start.11 = (s16[65,16,128]{2,1,0:T(8,128)(2,1)S(1)}, s16[65,16,128]{2,1,0:T(8,128)(2,1)S(1)}, u32[]{:S(2)}, u32[]{:S(2)}) collective-permute-start(s16[65,16,128]{2,1,0:T(8,128)(2,1)S(1)} %get-tuple-element.56), channel_id=1, source_target_pairs={{0,4},{4,0},{8,12},{12,8},{16,20},{20,16},{24,28},{28,24},{32,36},... | collective-permute-start | bytes 798728 | tf_op jit(solution)/shard_map/ppermute | solution.py:380
  128.8 9.8 %collective-permute-start.12 = (s16[65,16,128]{2,1,0:T(8,128)(2,1)S(1)}, s16[65,16,128]{2,1,0:T(8,128)(2,1)S(1)}, u32[]{:S(2)}, u32[]{:S(2)}) collective-permute-start(s16[65,16,128]{2,1,0:T(8,128)(2,1)S(1)} %get-tuple-element.57), channel_id=1, source_target_pairs={{4,8},{12,16},{20,24},{28,32},{36,40},{44,48},{52,56},{60,64},{68,... | collective-permute-start | bytes 798728 | tf_op jit(solution)/shard_map/ppermute | solution.py:386
  139.4 5.1 %collective-permute-start.13 = (s16[17,32,128]{2,1,0:T(8,128)(2,1)S(1)}, s16[17,32,128]{2,1,0:T(8,128)(2,1)S(1)}, u32[]{:S(2)}, u32[]{:S(2)}) collective-permute-start(s16[17,32,128]{2,1,0:T(8,128)(2,1)S(1)} %get-tuple-element.59), channel_id=1, source_target_pairs={{0,1},{1,0},{2,3},{3,2},{4,5},{5,4},{6,7},{7,6},{8,9},{9,8},{10,11... | collective-permute-start | bytes 417800 | tf_op jit(solution)/shard_map/ppermute | solution.py:380
  140.1 4.4 %collective-permute-start.14 = (s16[17,32,128]{2,1,0:T(8,128)(2,1)S(1)}, s16[17,32,128]{2,1,0:T(8,128)(2,1)S(1)}, u32[]{:S(2)}, u32[]{:S(2)}) collective-permute-start(s16[17,32,128]{2,1,0:T(8,128)(2,1)S(1)} %get-tuple-element.60), channel_id=1, source_target_pairs={{1,2},{2,1},{5,6},{6,5},{9,10},{10,9},{13,14},{14,13},{17,18},{18,... | collective-permute-start | bytes 417800 | tf_op jit(solution)/shard_map/ppermute | solution.py:386
  145.0 7.5 %collective-permute-start.15 = (s16[17,32,128]{2,1,0:T(8,128)(2,1)S(1)}, s16[17,32,128]{2,1,0:T(8,128)(2,1)S(1)}, u32[]{:S(2)}, u32[]{:S(2)}) collective-permute-start(s16[17,32,128]{2,1,0:T(8,128)(2,1)S(1)} %get-tuple-element.61.refs_0_), channel_id=1, source_target_pairs={{1,2},{3,0},{2,1},{0,3},{5,6},{7,4},{6,5},{4,7},{9,10},{11,8},{10,... | collective-permute-start | bytes 417800 | tf_op jit(solution)/shard_map/ppermute | solution.py:386
  146.5 8.4 %collective-permute-start.17 = (s16[17,32,128]{2,1,0:T(8,128)(2,1)S(1)}, s16[17,32,128]{2,1,0:T(8,128)(2,1)S(1)}, u32[]{:S(2)}, u32[]{:S(2)}) collective-permute-start(s16[17,32,128]{2,1,0:T(8,128)(2,1)S(1)} %get-tuple-element.62.refs_1_), channel_id=1, source_target_pairs={{0,1},{1,0},{2,3},{3,2},{4,5},{5,4},{6,7},{7,6},{8,9},{9,8},{10,11... | collective-permute-start | bytes 417800 | tf_op jit(solution)/shard_map/ppermute | solution.py:380
  149.8 6.3 %collective-permute-start.19 = (s16[17,32,128]{2,1,0:T(8,128)(2,1)S(1)}, s16[17,32,128]{2,1,0:T(8,128)(2,1)S(1)}, u32[]{:S(2)}, u32[]{:S(2)}) collective-permute-start(s16[17,32,128]{2,1,0:T(8,128)(2,1)S(1)} %get-tuple-element.61.refs_0_), channel_id=1, source_target_pairs={{0,1},{1,0},{2,3},{3,2},{4,5},{5,4},{6,7},{7,6},{8,9},{9,8},{10,11... | collective-permute-start | bytes 417800 | tf_op jit(solution)/shard_map/ppermute | solution.py:380
  149.8 6.8 %collective-permute-start.20 = (s16[17,32,128]{2,1,0:T(8,128)(2,1)S(1)}, s16[17,32,128]{2,1,0:T(8,128)(2,1)S(1)}, u32[]{:S(2)}, u32[]{:S(2)}) collective-permute-start(s16[17,32,128]{2,1,0:T(8,128)(2,1)S(1)} %get-tuple-element.62.refs_1_), channel_id=1, source_target_pairs={{1,2},{3,0},{2,1},{0,3},{5,6},{7,4},{6,5},{4,7},{9,10},{11,8},{10,... | collective-permute-start | bytes 417800 | tf_op jit(solution)/shard_map/ppermute | solution.py:386
  152.4 6.0 %collective-permute-start.16 = (s16[17,32,128]{2,1,0:T(8,128)(2,1)S(1)}, s16[17,32,128]{2,1,0:T(8,128)(2,1)S(1)}, u32[]{:S(2)}, u32[]{:S(2)}) collective-permute-start(s16[17,32,128]{2,1,0:T(8,128)(2,1)S(1)} %collective-permute-done.15.refs_4_), channel_id=1, source_target_pairs={{0,1},{1,0},{2,3},{3,2},{4,5},{5,4},{6,7},{7,6},{8,9},{9,8},{10,11... | collective-permute-start | bytes 417800 | tf_op jit(solution)/shard_map/ppermute | solution.py:380
  154.9 6.3 %collective-permute-start.18 = (s16[17,32,128]{2,1,0:T(8,128)(2,1)S(1)}, s16[17,32,128]{2,1,0:T(8,128)(2,1)S(1)}, u32[]{:S(2)}, u32[]{:S(2)}) collective-permute-start(s16[17,32,128]{2,1,0:T(8,128)(2,1)S(1)} %collective-permute-done.17.refs_3_), channel_id=1, source_target_pairs={{1,2},{3,0},{2,1},{0,3},{5,6},{7,4},{6,5},{4,7},{9,10},{11,8},{10,... | collective-permute-start | bytes 417800 | tf_op jit(solution)/shard_map/ppermute | solution.py:386
  (3 other events, 4.5 us)
where the time goes:
time: 163 us; the launch traced here: 162 us
  waiting for transfers between devices  69.8 us (43%)
  starting transfers between devices  47.8 us (29%)
  Pallas kernels  34.1 us (21%)
  local copies, waits for them, and re-layouts  6.14 us (4%)
  other arithmetic  2.44 us (1%)
    all_to_all x1, waiting for transfers between devices, per_device(): got = lax.all_to_all(sending, BOTH, 0, 0, tiled=True)  41.4 us
    pallas_call x10, Pallas kernels, call(): pl.pallas_call(kernel, out_shape=out_shape, in_specs=[SMEM] * scalars + [...  33.2 us
    ppermute x10, starting transfers between devices, swap_far(): return lax.ppermute(a, axis, pairs + [(j, i) for i, j in pairs])  27.4 us
    ppermute x10, waiting for transfers between devices, swap_near(): lax.ppermute(a, axis, [(i, i ^ 1) for i in range(lax.axis_size(axis))])  15.7 us
    ppermute x10, waiting for transfers between devices, swap_far(): return lax.ppermute(a, axis, pairs + [(j, i) for i, j in pairs])  12.7 us
    all_to_all x1, starting transfers between devices, per_device(): got = lax.all_to_all(sending, BOTH, 0, 0, tiled=True)  10.6 us
    ppermute x10, starting transfers between devices, swap_near(): lax.ppermute(a, axis, [(i, i ^ 1) for i in range(lax.axis_size(axis))])  8.25 us
    unnamed x10, local copies, waits for them, and re-layouts  4.51 us
  transfers between devices with their start and end apart: 22, of which 9 were waited for; matrix products, arithmetic and copies ran while one was open for 3% of the time, Pallas kernels for 7%

commit v1 on v0

--- a/solution.py
+++ b/solution.py
@@ -144,6 +144,14 @@
 def for_parity(odd, body):
     for value in (0, 1):
         pl.when(odd == value)(partial(body, value))
+
+
+def send_x(part, near, far):
+    def send(odd):
+        x_near, x_far = sides(odd, part.shape[1] - near.shape[1])
+        send_part(part, (near, 0, x_near), (far, 0, x_far))
+
+    for_parity(odd_of("brick"), send)
 
 
 def prepare_kernel(estimate, middle, near, far):
@@ -204,46 +212,46 @@
     return (data / den.astype(F32)).astype(BF16)
 
 
-def back_kernel(where, blurred, got, axt, ayt, tzt, out, nn, fn, nf, ff, t1):
+def back_kernel(where, blurred, got, axt, ayt, tzt, out, send_near, send_far, t1):
     views, core = ayt.shape[0], got.shape[1]
     back_steps(
         lambda v: ratio_rows(v, core, where, got, blurred[v]), axt, ayt, tzt, t1, out, views, core
     )
-    y_near, y_far = sides(odd_of("view"), out.shape[0] // 2)
-
-    def send(odd):
-        x_near, x_far = sides(odd, out.shape[1] - nn.shape[1])
-        send_part(
-            out, (nn, y_near, x_near), (fn, y_near, x_far), (nf, y_far, x_near), (ff, y_far, x_far)
-        )
-
-    for_parity(odd_of("brick"), send)
+    send_x(out, send_near, send_far)
 
 
 def full_kernel(
-    where, near, middle, far, total_near, total_far, got_near, got_far,
+    where, near, middle, far, total_near, total_far, got_nn, got_nf, got_fn, got_ff,
     got, ax, ay, tz, axt, ayt, tzt, kept, out, send_near, send_far, fe, t1, ratios,
 ):
     views, core = ay.shape[0], ay.shape[1]
     y_near, y_far = sides(odd_of("view"), out.shape[0] // 2)
 
     def renew(odd):
-        x_near, x_far = sides(odd, REACH + core)
-        fields = (near, x_near, REACH), (far, x_far, REACH), (middle, REACH, core)
-        for codes, total, first in ((got_near, total_near, y_near), (got_far, total_far, y_far)):
-            scale = scale_of(codes)
-
-            def block(y):
-                rows, here = pl.ds(first + y, 8), pl.ds(y, 8)
-                for field, x, width in fields:
-                    cells = slice(x, x + width)
-                    step = (total[here, cells] + decode(codes[here, cells], scale)) / views
-                    fresh = field[rows].astype(F32) * step
-                    fe[rows, cells] = fresh.astype(BF16)
-                    if field is middle:
-                        kept[rows] = fresh
-
-            in_blocks(total.shape[0], block)
+        columns = zip(
+            sides(odd, core),
+            sides(odd, REACH + core),
+            (near, far),
+            (total_near, total_far),
+            ((got_nn, got_nf), (got_fn, got_ff)),
+        )
+        for start, x_outer, outer, total, messages in columns:
+            x_inner = 2 * start + REACH - x_outer
+            inner = middle.at[:, x_inner - REACH : x_inner]
+            for codes, first in zip(messages, (y_near, y_far)):
+                scale = scale_of(codes)
+
+                def block(y):
+                    rows, here = pl.ds(first + y, 8), pl.ds(y, 8)
+                    for x, field in ((x_outer, outer), (x_inner, inner)):
+                        cells = slice(x - start, x - start + REACH)
+                        step = (total[rows, cells] + decode(codes[here, cells], scale)) / views
+                        fresh = field[rows].astype(F32) * step
+                        fe[rows, x : x + REACH] = fresh.astype(BF16)
+                        if field is inner:
+                            kept[rows, x - REACH : x] = fresh
+
+                in_blocks(codes.shape[0] - 1, block)
 
     for_parity(odd_of("brick"), renew)
 
@@ -252,15 +260,27 @@
 
     blur_steps(fe, ax, ay, tz, t1, views, core, finish)
     back_steps(lambda v: ratios[v], axt, ayt, tzt, t1, out, views, core)
-
-    def send(odd):
-        x_near, x_far = sides(odd, out.shape[1] - REACH)
-        send_part(out, (send_near, 0, x_near), (send_far, 0, x_far))
-
-    for_parity(odd_of("brick"), send)
-
-
-def gather_rows(first, part, near, far, out):
+    send_x(out, send_near, send_far)
+
+
+def gather_side_kernel(which, part, got, out, send_near, send_far):
+    scale, side = scale_of(got), got.shape[1]
+
+    def add(odd):
+        x = sides(odd, side)[which]
+
+        def block(y):
+            rows = pl.ds(y, 8)
+            out[rows] = part[rows, x : x + side] + decode(got[rows], scale)
+
+        in_blocks(out.shape[0], block)
+
+    for_parity(odd_of("brick"), add)
+    y_near, y_far = sides(odd_of("view"), out.shape[0] // 2)
+    send_part(out, (send_near, y_near, 0), (send_far, y_far, 0))
+
+
+def gather_kernel(part, near, far, out, send_near, send_far):
     side = near.shape[1]
     off = (part.shape[1] - 2 * side) // 2
     scale_n, scale_f = scale_of(near), scale_of(far)
@@ -271,23 +291,13 @@
         def block(y):
             rows = pl.ds(y, 8)
             for got, scale, x in ((near, scale_n, x_near), (far, scale_f, x_far)):
-                here = part[pl.ds(first + y, 8), off + x : off + x + side]
+                here = part[rows, off + x : off + x + side]
                 out[rows, x : x + side] = here + decode(got[rows], scale)
 
         in_blocks(out.shape[0], block)
 
     for_parity(odd_of("brick"), add_both)
-
-
-def gather_half_kernel(which, part, near, far, out, message):
-    first = sides(odd_of("view"), part.shape[0] // 2)[which]
-    gather_rows(first, part, near, far, out)
-    send_part(out, (message, 0, 0))
-
-
-def gather_all_kernel(part, near, far, out, send_near, send_far):
-    gather_rows(0, part, near, far, out)
-    y_near, y_far = sides(odd_of("view"), part.shape[0] - REACH)
+    y_near, y_far = sides(odd_of("view"), out.shape[0] - send_near.shape[0] + 1)
     send_part(out, (send_near, y_near, 0), (send_far, y_far, 0))
 
 
@@ -475,9 +485,9 @@
         *forward,
     )
     side = 2 * REACH
-    part, nn, fn, nf, ff = call(
+    part, send_near, send_far = call(
         back_kernel,
-        (shape(ext, ext),) + (codes(side + 1, side),) * 4,
+        (shape(ext, ext),) + (codes(ext + 1, side),) * 2,
         [scratch],
         flops,
         where,
@@ -486,15 +496,10 @@
         *back,
         scalars=1,
     )
-    parts = swap_near(nn, "brick"), swap_far(fn, "brick")
-    others = swap_near(nf, "brick"), swap_far(ff, "brick")
-    half_shape = (shape(side, ext), codes(side + 1, ext))
-    total_near, send_near = call(
-        partial(gather_half_kernel, 0), half_shape, [], 0, part, *parts
-    )
-    total_far, send_far = call(
-        partial(gather_half_kernel, 1), half_shape, [], 0, part, *others
-    )
+    side_shape = (shape(ext, side),) + (codes(side + 1, side),) * 2
+    from_far, from_near = swap_far(send_far, "brick"), swap_near(send_near, "brick")
+    total_near, nn, nf = call(partial(gather_side_kernel, 0), side_shape, [], 0, part, from_near)
+    total_far, fn, ff = call(partial(gather_side_kernel, 1), side_shape, [], 0, part, from_far)
     side = REACH
     kept, part, send_near, send_far = call(
         full_kernel,
@@ -505,15 +510,17 @@
         *field,
         total_near,
         total_far,
-        swap_near(send_near, "view"),
-        swap_far(send_far, "view"),
+        swap_near(nn, "view"),
+        swap_far(nf, "view"),
+        swap_near(fn, "view"),
+        swap_far(ff, "view"),
         got,
         *forward,
         *back,
         scalars=1,
     )
     total, send_near, send_far = call(
-        gather_all_kernel,
+        gather_kernel,
         (shape(ext, planes), codes(side + 1, planes), codes(side + 1, planes)),
         [],
         0,

time: 163 us -> 164 us (level)
    ppermute x10, waiting for transfers between devices: 15.7 us -> 8.54 us  [swap_near(): lax.ppermute(a, axis, [(i, i ^ 1) for i in range(lax.axis_size(axis))])]
    ppermute x10, starting transfers between devices: 8.25 us -> 15.1 us  [swap_near(): lax.ppermute(a, axis, [(i, i ^ 1) for i in range(lax.axis_size(axis))])]
    ppermute x10, waiting for transfers between devices: 12.7 us -> 19.3 us  [swap_far(): return lax.ppermute(a, axis, pairs + [(j, i) for i, j in pairs])]
    ppermute x10, starting transfers between devices: 27.4 us -> 22 us  [swap_far(): return lax.ppermute(a, axis, pairs + [(j, i) for i, j in pairs])]
  transfers between devices with their start and end apart: 22 -> 22, of which waited for: 9 -> 8; matrix products, arithmetic and copies ran while one was open for 3% -> 3% of each run, Pallas kernels for 7% -> 7%
where the time goes in v1:
time: 164 us; the launch traced here: 163 us
  waiting for transfers between devices  69.2 us (42%)
  starting transfers between devices  49.2 us (30%)
  Pallas kernels  34.2 us (21%)
  local copies, waits for them, and re-layouts  6.14 us (4%)
  other arithmetic  2.44 us (1%)
    all_to_all x1, waiting for transfers between devices, per_device(): got = lax.all_to_all(sending, BOTH, 0, 0, tiled=True)  41.4 us
    pallas_call x10, Pallas kernels, call(): pl.pallas_call(kernel, out_shape=out_shape, in_specs=[SMEM] * scalars + [...  33.3 us
    ppermute x10, starting transfers between devices, swap_far(): return lax.ppermute(a, axis, pairs + [(j, i) for i, j in pairs])  22 us
    ppermute x10, waiting for transfers between devices, swap_far(): return lax.ppermute(a, axis, pairs + [(j, i) for i, j in pairs])  19.3 us
    ppermute x10, starting transfers between devices, swap_near(): lax.ppermute(a, axis, [(i, i ^ 1) for i in range(lax.axis_size(axis))])  15.1 us
    all_to_all x1, starting transfers between devices, per_device(): got = lax.all_to_all(sending, BOTH, 0, 0, tiled=True)  10.6 us
    ppermute x10, waiting for transfers between devices, swap_near(): lax.ppermute(a, axis, [(i, i ^ 1) for i in range(lax.axis_size(axis))])  8.54 us
    unnamed x10, local copies, waits for them, and re-layouts  4.51 us
  transfers between devices with their start and end apart: 22, of which 8 were waited for; matrix products, arithmetic and copies ran while one was open for 3% of the time, Pallas kernels for 7%

profile of v1, /device:TPU:2, one launch (start us, length us, event | category | flops | bytes accessed | tf_op | source)
XLA Modules:
  0.0 163.1 jit_solution(9615796836033741752)
XLA Ops:
  0.0 1.6 copy-done
  2.5 3.0 %collective-permute-start.3 = (f32[2,128]{1,0:T(2,128)S(1)}, f32[2,128]{1,0:T(2,128)S(1)}, u32[]{:S(2)}, u32[]{:S(2)}) collective-permute-start(f32[2,128]{1,0:T(2,128)S(1)} %select_maximum_fusion), channel_id=1, source_target_pairs={{1,2},{3,0},{2,1},{0,3},{5,6},{7,4},{6,5},{4,7},{9,10},{11,8},{10,... | collective-permute-start | bytes 3080 | tf_op jit(solution)/shard_map/ppermute | solution.py:396
  7.2 6.0 %collective-permute-start.1 = (bf16[64,16,128]{2,1,0:T(8,128)(2,1)S(1)}, bf16[64,16,128]{2,1,0:T(8,128)(2,1)S(1)}, u32[]{:S(2)}, u32[]{:S(2)}) collective-permute-start(bf16[64,16,128]{2,1,0:T(8,128)(2,1)S(1)} %get-tuple-element.37), channel_id=1, source_target_pairs={{4,8},{12,16},{20,24},{28,32},{36,40},{44,48},{52,56},{60,64},{68,... | collective-permute-start | bytes 786440 | tf_op jit(solution)/shard_map/ppermute | solution.py:396
  13.4 3.8 %shard_map.46 = bf16[32,4,2,2,32,128]{5,4,3,2,1,0:T(8,128)(2,1)} custom-call(bf16[2,32,2,128,128]{4,3,2,1,0:T(8,128)(2,1)} %bitcast.44), custom_call_target="tpu_custom_call" | custom-call | bytes 4194304 | tf_op jit(solution)/shard_map/pallas_call | solution.py:367
  17.4 10.6 %all-to-all-start = ((bf16[128,4,32,128]{3,2,1,0:T(8,128)(2,1)}), bf16[128,4,32,128]{3,2,1,0:T(8,128)(2,1)}, u32[]{:S(2)}, u32[]{:S(2)}) async-start(bf16[128,4,32,128]{3,2,1,0:T(8,128)(2,1)} %bitcast.43), calls=%async_computation | async-start | bytes 8388608 | tf_op jit(solution)/shard_map/all_to_all | solution.py:455
  32.6 4.5 %shard_map.48.blurred = bf16[8,1024,128]{2,1,0:T(8,128)(2,1)S(1)} custom-call(bf16[64,16,128]{2,1,0:T(8,128)(2,1)S(1)} %collective-permute-done.near, f32[64,32,128]{2,1,0:T(8,128)S(1)} %get-tuple-element.42.middle, bf16[64,16,128]{2,1,0:T(8,128)(2,1)S(1)} %collective-permute-done.1.far, bf16[256,128]{1,0:T(8,128)(2,1)S(1)} %pad_maximum_fusion.3.ax, ...), custom_call_target="tpu_custom_call" | custom-call | flops 4000000000 | bytes 2228224 | tf_op jit(solution)/shard_map/pallas_call | solution.py:367
  38.5 41.4 %all-to-all-done = bf16[128,4,32,128]{3,2,1,0:T(8,128)(2,1)} async-done(((bf16[128,4,32,128]{3,2,1,0:T(8,128)(2,1)}), bf16[128,4,32,128]{3,2,1,0:T(8,128)(2,1)}, u32[]{:S(2)}, u32[]{:S(2)}) %all-to-all-start) | async-done | bytes 4194336 | tf_op jit(solution)/shard_map/all_to_all | solution.py:455
  81.5 7.9 %shard_map.49 = (f32[64,64,128]{2,1,0:T(8,128)S(1)}, s16[65,32,128]{2,1,0:T(8,128)(2,1)S(1)}, s16[65,32,128]{2,1,0:T(8,128)(2,1)S(1)}) custom-call(s32[256]{0:T(256)S(1)} %reshape.94.where, bf16[8,1024,128]{2,1,0:T(8,128)(2,1)S(1)} %copy-done.2, bf16[512,32,128]{2,1,0:T(8,128)(2,1)} %bitcast.21.got, bf16[128,256]{1,0:T(8,128)(2,1)S(1)} %pad_maximum_fusion.5.axt, ...), custom_call_target="tpu_custom_call" | custom-call | flops 4000000000 | bytes 6947840 | tf_op jit(solution)/shard_map/pallas_call | solution.py:367
  89.4 3.0 %collective-permute-start.6 = (s16[65,32,128]{2,1,0:T(8,128)(2,1)S(1)}, s16[65,32,128]{2,1,0:T(8,128)(2,1)S(1)}, u32[]{:S(2)}, u32[]{:S(2)}) collective-permute-start(s16[65,32,128]{2,1,0:T(8,128)(2,1)S(1)} %get-tuple-element.48), channel_id=1, source_target_pairs={{4,8},{12,16},{20,24},{28,32},{36,40},{44,48},{52,56},{60,64},{68,... | collective-permute-start | bytes 1597448 | tf_op jit(solution)/shard_map/ppermute | solution.py:396
  92.4 9.6 %collective-permute-done.6.got = s16[65,32,128]{2,1,0:T(8,128)(2,1)S(1)} collective-permute-done((s16[65,32,128]{2,1,0:T(8,128)(2,1)S(1)}, s16[65,32,128]{2,1,0:T(8,128)(2,1)S(1)}, u32[]{:S(2)}, u32[]{:S(2)}) %collective-permute-start.6) | collective-permute-done | bytes 532512 | tf_op jit(solution)/shard_map/ppermute | solution.py:396
  105.0 3.8 %collective-permute-start.7 = (s16[33,32,128]{2,1,0:T(8,128)(2,1)S(1)}, s16[33,32,128]{2,1,0:T(8,128)(2,1)S(1)}, u32[]{:S(2)}, u32[]{:S(2)}) collective-permute-start(s16[33,32,128]{2,1,0:T(8,128)(2,1)S(1)} %get-tuple-element.50), channel_id=1, source_target_pairs={{0,1},{1,0},{2,3},{3,2},{4,5},{5,4},{6,7},{7,6},{8,9},{9,8},{10,11... | collective-permute-start | bytes 811016 | tf_op jit(solution)/shard_map/ppermute | solution.py:390
  109.5 2.9 %collective-permute-done.9.got_fn = s16[33,32,128]{2,1,0:T(8,128)(2,1)S(1)} collective-permute-done((s16[33,32,128]{2,1,0:T(8,128)(2,1)S(1)}, s16[33,32,128]{2,1,0:T(8,128)(2,1)S(1)}, u32[]{:S(2)}, u32[]{:S(2)}) %collective-permute-start.9) | collective-permute-done | bytes 270368 | tf_op jit(solution)/shard_map/ppermute | solution.py:390
  112.4 3.3 %collective-permute-done.7.got_nn = s16[33,32,128]{2,1,0:T(8,128)(2,1)S(1)} collective-permute-done((s16[33,32,128]{2,1,0:T(8,128)(2,1)S(1)}, s16[33,32,128]{2,1,0:T(8,128)(2,1)S(1)}, u32[]{:S(2)}, u32[]{:S(2)}) %collective-permute-start.7) | collective-permute-done | bytes 270368 | tf_op jit(solution)/shard_map/ppermute | solution.py:390
  115.7 12.3 %shard_map.52 = (f32[64,32,128]{2,1,0:T(8,128)S(1)}, f32[64,64,128]{2,1,0:T(8,128)S(1)}, s16[65,16,128]{2,1,0:T(8,128)(2,1)S(1)}, s16[65,16,128]{2,1,0:T(8,128)(2,1)S(1)}) custom-call(s32[256]{0:T(256)S(1)} %reshape.94.where, bf16[64,16,128]{2,1,0:T(8,128)(2,1)S(1)} %collective-permute-done.near, f32[64,32,128]{2,1,0:T(8,128)S(1)} %get-tuple-element.42.middle, ...), custom_call_target="tpu_custom_call" | custom-call | flops 8000000000 | bytes 10257408 | tf_op jit(solution)/shard_map/pallas_call | solution.py:367
  128.1 3.0 %collective-permute-start.12 = (s16[65,16,128]{2,1,0:T(8,128)(2,1)S(1)}, s16[65,16,128]{2,1,0:T(8,128)(2,1)S(1)}, u32[]{:S(2)}, u32[]{:S(2)}) collective-permute-start(s16[65,16,128]{2,1,0:T(8,128)(2,1)S(1)} %get-tuple-element.57), channel_id=1, source_target_pairs={{4,8},{12,16},{20,24},{28,32},{36,40},{44,48},{52,56},{60,64},{68,... | collective-permute-start | bytes 798728 | tf_op jit(solution)/shard_map/ppermute | solution.py:396
  131.1 6.9 %collective-permute-done.12.far = s16[65,16,128]{2,1,0:T(8,128)(2,1)S(1)} collective-permute-done((s16[65,16,128]{2,1,0:T(8,128)(2,1)S(1)}, s16[65,16,128]{2,1,0:T(8,128)(2,1)S(1)}, u32[]{:S(2)}, u32[]{:S(2)}) %collective-permute-start.12) | collective-permute-done | bytes 266272 | tf_op jit(solution)/shard_map/ppermute | solution.py:396
  138.6 3.7 %collective-permute-start.13 = (s16[17,32,128]{2,1,0:T(8,128)(2,1)S(1)}, s16[17,32,128]{2,1,0:T(8,128)(2,1)S(1)}, u32[]{:S(2)}, u32[]{:S(2)}) collective-permute-start(s16[17,32,128]{2,1,0:T(8,128)(2,1)S(1)} %get-tuple-element.59), channel_id=1, source_target_pairs={{0,1},{1,0},{2,3},{3,2},{4,5},{5,4},{6,7},{7,6},{8,9},{9,8},{10,11... | collective-permute-start | bytes 417800 | tf_op jit(solution)/shard_map/ppermute | solution.py:390
  143.0 2.4 %collective-permute-done.13.near = s16[17,32,128]{2,1,0:T(8,128)(2,1)S(1)} collective-permute-done((s16[17,32,128]{2,1,0:T(8,128)(2,1)S(1)}, s16[17,32,128]{2,1,0:T(8,128)(2,1)S(1)}, u32[]{:S(2)}, u32[]{:S(2)}) %collective-permute-start.13) | collective-permute-done | bytes 139296 | tf_op jit(solution)/shard_map/ppermute | solution.py:390
  147.4 3.3 %collective-permute-start.17 = (s16[17,32,128]{2,1,0:T(8,128)(2,1)S(1)}, s16[17,32,128]{2,1,0:T(8,128)(2,1)S(1)}, u32[]{:S(2)}, u32[]{:S(2)}) collective-permute-start(s16[17,32,128]{2,1,0:T(8,128)(2,1)S(1)} %get-tuple-element.62.refs_1_), channel_id=1, source_target_pairs={{0,1},{1,0},{2,3},{3,2},{4,5},{5,4},{6,7},{7,6},{8,9},{9,8},{10,11... | collective-permute-start | bytes 417800 | tf_op jit(solution)/shard_map/ppermute | solution.py:390
  150.8 1.8 %collective-permute-start.20 = (s16[17,32,128]{2,1,0:T(8,128)(2,1)S(1)}, s16[17,32,128]{2,1,0:T(8,128)(2,1)S(1)}, u32[]{:S(2)}, u32[]{:S(2)}) collective-permute-start(s16[17,32,128]{2,1,0:T(8,128)(2,1)S(1)} %get-tuple-element.62.refs_1_), channel_id=1, source_target_pairs={{1,2},{3,0},{2,1},{0,3},{5,6},{7,4},{6,5},{4,7},{9,10},{11,8},{10,... | collective-permute-start | bytes 417800 | tf_op jit(solution)/shard_map/ppermute | solution.py:396
  152.6 3.2 %collective-permute-start.16 = (s16[17,32,128]{2,1,0:T(8,128)(2,1)S(1)}, s16[17,32,128]{2,1,0:T(8,128)(2,1)S(1)}, u32[]{:S(2)}, u32[]{:S(2)}) collective-permute-start(s16[17,32,128]{2,1,0:T(8,128)(2,1)S(1)} %collective-permute-done.15.refs_4_), channel_id=1, source_target_pairs={{0,1},{1,0},{2,3},{3,2},{4,5},{5,4},{6,7},{7,6},{8,9},{9,8},{10,11... | collective-permute-start | bytes 417800 | tf_op jit(solution)/shard_map/ppermute | solution.py:390
  155.8 1.7 %collective-permute-start.18 = (s16[17,32,128]{2,1,0:T(8,128)(2,1)S(1)}, s16[17,32,128]{2,1,0:T(8,128)(2,1)S(1)}, u32[]{:S(2)}, u32[]{:S(2)}) collective-permute-start(s16[17,32,128]{2,1,0:T(8,128)(2,1)S(1)} %collective-permute-done.17.refs_3_), channel_id=1, source_target_pairs={{1,2},{3,0},{2,1},{0,3},{5,6},{7,4},{6,5},{4,7},{9,10},{11,8},{10,... | collective-permute-start | bytes 417800 | tf_op jit(solution)/shard_map/ppermute | solution.py:396
  158.1 1.8 %shard_map.55._ = f32[32,128,128]{2,1,0:T(8,128)} custom-call(s16[17,32,128]{2,1,0:T(8,128)(2,1)S(1)} %get-tuple-element.61.refs_0_, s16[17,32,128]{2,1,0:T(8,128)(2,1)S(1)} %get-tuple-element.62.refs_1_, s16[17,32,128]{2,1,0:T(8,128)(2,1)S(1)} %collective-permute-done.19.refs_2_, s16[17,32,128]{2,1,0:T(8,128)(2,1)S(1)} %collective-permute-done.17.refs_3_, ...), custom_call_target="tpu_custom_call" | custom-call | bytes 835584 | tf_op jit(solution)/shard_map/pallas_call | solution.py:367
  159.9 2.2 %collective-permute-done.18.upper = s16[17,32,128]{2,1,0:T(8,128)(2,1)S(1)} collective-permute-done((s16[17,32,128]{2,1,0:T(8,128)(2,1)S(1)}, s16[17,32,128]{2,1,0:T(8,128)(2,1)S(1)}, u32[]{:S(2)}, u32[]{:S(2)}) %collective-permute-start.18) | collective-permute-done | bytes 139296 | tf_op jit(solution)/shard_map/ppermute | solution.py:396
  (84 shorter events, 19.0 us)
Async XLA Ops:
  0.0 2.2 %copy-start.4 = (s32[2,1024,1]{1,2,0:T(1,128)S(1)}, s32[2,1024,1]{1,2,0:T(1,128)}, u32[]{:S(2)}) copy-start(s32[2,1024,1]{1,2,0:T(1,128)} %param.7) | copy-start | bytes 24580
  0.0 1.9 %copy-start.3 = (f32[2,3,31]{2,0,1:T(2,128)S(1)}, f32[2,3,31]{2,0,1:T(2,128)}, u32[]{:S(2)}) copy-start(f32[2,3,31]{2,0,1:T(2,128)} %param.6) | copy-start | bytes 2236
  2.5 14.7 %collective-permute-start.3 = (f32[2,128]{1,0:T(2,128)S(1)}, f32[2,128]{1,0:T(2,128)S(1)}, u32[]{:S(2)}, u32[]{:S(2)}) collective-permute-start(f32[2,128]{1,0:T(2,128)S(1)} %select_maximum_fusion), channel_id=1, source_target_pairs={{1,2},{3,0},{2,1},{0,3},{5,6},{7,4},{6,5},{4,7},{9,10},{11,8},{10,... | collective-permute-start | bytes 3080 | tf_op jit(solution)/shard_map/ppermute | solution.py:396
  5.5 11.7 %collective-permute-start.2 = (f32[2,128]{1,0:T(2,128)S(1)}, f32[2,128]{1,0:T(2,128)S(1)}, u32[]{:S(2)}, u32[]{:S(2)}) collective-permute-start(f32[2,128]{1,0:T(2,128)S(1)} %select_maximum_fusion), channel_id=1, source_target_pairs={{0,1},{1,0},{2,3},{3,2},{4,5},{5,4},{6,7},{7,6},{8,9},{9,8},{10,11... | collective-permute-start | bytes 3080 | tf_op jit(solution)/shard_map/ppermute | solution.py:390
  5.7 11.6 %collective-permute-start.4 = (f32[2,128]{1,0:T(2,128)S(1)}, f32[2,128]{1,0:T(2,128)S(1)}, u32[]{:S(2)}, u32[]{:S(2)}) collective-permute-start(f32[2,128]{1,0:T(2,128)S(1)} %select_maximum_fusion), channel_id=1, source_target_pairs={{0,2},{1,3},{2,0},{3,1},{4,6},{5,7},{6,4},{7,5},{8,10},{9,11},{10,... | collective-permute-start | bytes 3080 | tf_op jit(solution)/shard_map/ppermute | solution.py:434
  7.2 10.1 %collective-permute-start = (bf16[64,16,128]{2,1,0:T(8,128)(2,1)S(1)}, bf16[64,16,128]{2,1,0:T(8,128)(2,1)S(1)}, u32[]{:S(2)}, u32[]{:S(2)}) collective-permute-start(bf16[64,16,128]{2,1,0:T(8,128)(2,1)S(1)} %get-tuple-element.36), channel_id=1, source_target_pairs={{0,4},{4,0},{8,12},{12,8},{16,20},{20,16},{24,28},{28,24},{32,36},... | collective-permute-start | bytes 786440 | tf_op jit(solution)/shard_map/ppermute | solution.py:390
  7.2 10.1 %collective-permute-start.1 = (bf16[64,16,128]{2,1,0:T(8,128)(2,1)S(1)}, bf16[64,16,128]{2,1,0:T(8,128)(2,1)S(1)}, u32[]{:S(2)}, u32[]{:S(2)}) collective-permute-start(bf16[64,16,128]{2,1,0:T(8,128)(2,1)S(1)} %get-tuple-element.37), channel_id=1, source_target_pairs={{4,8},{12,16},{20,24},{28,32},{36,40},{44,48},{52,56},{60,64},{68,... | collective-permute-start | bytes 786440 | tf_op jit(solution)/shard_map/ppermute | solution.py:396
  17.4 62.5 %all-to-all-start = ((bf16[128,4,32,128]{3,2,1,0:T(8,128)(2,1)}), bf16[128,4,32,128]{3,2,1,0:T(8,128)(2,1)}, u32[]{:S(2)}, u32[]{:S(2)}) async-start(bf16[128,4,32,128]{3,2,1,0:T(8,128)(2,1)} %bitcast.43), calls=%async_computation | async-start | bytes 8388608 | tf_op jit(solution)/shard_map/all_to_all | solution.py:455
  89.4 12.7 %collective-permute-start.6 = (s16[65,32,128]{2,1,0:T(8,128)(2,1)S(1)}, s16[65,32,128]{2,1,0:T(8,128)(2,1)S(1)}, u32[]{:S(2)}, u32[]{:S(2)}) collective-permute-start(s16[65,32,128]{2,1,0:T(8,128)(2,1)S(1)} %get-tuple-element.48), channel_id=1, source_target_pairs={{4,8},{12,16},{20,24},{28,32},{36,40},{44,48},{52,56},{60,64},{68,... | collective-permute-start | bytes 1597448 | tf_op jit(solution)/shard_map/ppermute | solution.py:396
  92.3 11.9 %collective-permute-start.5 = (s16[65,32,128]{2,1,0:T(8,128)(2,1)S(1)}, s16[65,32,128]{2,1,0:T(8,128)(2,1)S(1)}, u32[]{:S(2)}, u32[]{:S(2)}) collective-permute-start(s16[65,32,128]{2,1,0:T(8,128)(2,1)S(1)} %get-tuple-element.46), channel_id=1, source_target_pairs={{0,4},{4,0},{8,12},{12,8},{16,20},{20,16},{24,28},{28,24},{32,36},... | collective-permute-start | bytes 1597448 | tf_op jit(solution)/shard_map/ppermute | solution.py:390
  102.9 9.5 %collective-permute-start.9 = (s16[33,32,128]{2,1,0:T(8,128)(2,1)S(1)}, s16[33,32,128]{2,1,0:T(8,128)(2,1)S(1)}, u32[]{:S(2)}, u32[]{:S(2)}) collective-permute-start(s16[33,32,128]{2,1,0:T(8,128)(2,1)S(1)} %get-tuple-element.52), channel_id=1, source_target_pairs={{0,1},{1,0},{2,3},{3,2},{4,5},{5,4},{6,7},{7,6},{8,9},{9,8},{10,11... | collective-permute-start | bytes 811016 | tf_op jit(solution)/shard_map/ppermute | solution.py:390
  103.5 8.9 %collective-permute-start.10 = (s16[33,32,128]{2,1,0:T(8,128)(2,1)S(1)}, s16[33,32,128]{2,1,0:T(8,128)(2,1)S(1)}, u32[]{:S(2)}, u32[]{:S(2)}) collective-permute-start(s16[33,32,128]{2,1,0:T(8,128)(2,1)S(1)} %get-tuple-element.53), channel_id=1, source_target_pairs={{1,2},{2,1},{5,6},{6,5},{9,10},{10,9},{13,14},{14,13},{17,18},{18,... | collective-permute-start | bytes 811016 | tf_op jit(solution)/shard_map/ppermute | solution.py:396
  105.0 10.6 %collective-permute-start.7 = (s16[33,32,128]{2,1,0:T(8,128)(2,1)S(1)}, s16[33,32,128]{2,1,0:T(8,128)(2,1)S(1)}, u32[]{:S(2)}, u32[]{:S(2)}) collective-permute-start(s16[33,32,128]{2,1,0:T(8,128)(2,1)S(1)} %get-tuple-element.50), channel_id=1, source_target_pairs={{0,1},{1,0},{2,3},{3,2},{4,5},{5,4},{6,7},{7,6},{8,9},{9,8},{10,11... | collective-permute-start | bytes 811016 | tf_op jit(solution)/shard_map/ppermute | solution.py:390
  108.8 6.8 %collective-permute-start.8 = (s16[33,32,128]{2,1,0:T(8,128)(2,1)S(1)}, s16[33,32,128]{2,1,0:T(8,128)(2,1)S(1)}, u32[]{:S(2)}, u32[]{:S(2)}) collective-permute-start(s16[33,32,128]{2,1,0:T(8,128)(2,1)S(1)} %get-tuple-element.51), channel_id=1, source_target_pairs={{1,2},{2,1},{5,6},{6,5},{9,10},{10,9},{13,14},{14,13},{17,18},{18,... | collective-permute-start | bytes 811016 | tf_op jit(solution)/shard_map/ppermute | solution.py:396
  128.0 3.1 %collective-permute-start.11 = (s16[65,16,128]{2,1,0:T(8,128)(2,1)S(1)}, s16[65,16,128]{2,1,0:T(8,128)(2,1)S(1)}, u32[]{:S(2)}, u32[]{:S(2)}) collective-permute-start(s16[65,16,128]{2,1,0:T(8,128)(2,1)S(1)} %get-tuple-element.56), channel_id=1, source_target_pairs={{0,4},{4,0},{8,12},{12,8},{16,20},{20,16},{24,28},{28,24},{32,36},... | collective-permute-start | bytes 798728 | tf_op jit(solution)/shard_map/ppermute | solution.py:390
  128.1 9.8 %collective-permute-start.12 = (s16[65,16,128]{2,1,0:T(8,128)(2,1)S(1)}, s16[65,16,128]{2,1,0:T(8,128)(2,1)S(1)}, u32[]{:S(2)}, u32[]{:S(2)}) collective-permute-start(s16[65,16,128]{2,1,0:T(8,128)(2,1)S(1)} %get-tuple-element.57), channel_id=1, source_target_pairs={{4,8},{12,16},{20,24},{28,32},{36,40},{44,48},{52,56},{60,64},{68,... | collective-permute-start | bytes 798728 | tf_op jit(solution)/shard_map/ppermute | solution.py:396
  138.6 6.7 %collective-permute-start.13 = (s16[17,32,128]{2,1,0:T(8,128)(2,1)S(1)}, s16[17,32,128]{2,1,0:T(8,128)(2,1)S(1)}, u32[]{:S(2)}, u32[]{:S(2)}) collective-permute-start(s16[17,32,128]{2,1,0:T(8,128)(2,1)S(1)} %get-tuple-element.59), channel_id=1, source_target_pairs={{0,1},{1,0},{2,3},{3,2},{4,5},{5,4},{6,7},{7,6},{8,9},{9,8},{10,11... | collective-permute-start | bytes 417800 | tf_op jit(solution)/shard_map/ppermute | solution.py:390
  142.3 3.0 %collective-permute-start.14 = (s16[17,32,128]{2,1,0:T(8,128)(2,1)S(1)}, s16[17,32,128]{2,1,0:T(8,128)(2,1)S(1)}, u32[]{:S(2)}, u32[]{:S(2)}) collective-permute-start(s16[17,32,128]{2,1,0:T(8,128)(2,1)S(1)} %get-tuple-element.60), channel_id=1, source_target_pairs={{1,2},{2,1},{5,6},{6,5},{9,10},{10,9},{13,14},{14,13},{17,18},{18,... | collective-permute-start | bytes 417800 | tf_op jit(solution)/shard_map/ppermute | solution.py:396
  145.9 6.7 %collective-permute-start.15 = (s16[17,32,128]{2,1,0:T(8,128)(2,1)S(1)}, s16[17,32,128]{2,1,0:T(8,128)(2,1)S(1)}, u32[]{:S(2)}, u32[]{:S(2)}) collective-permute-start(s16[17,32,128]{2,1,0:T(8,128)(2,1)S(1)} %get-tuple-element.61.refs_0_), channel_id=1, source_target_pairs={{1,2},{3,0},{2,1},{0,3},{5,6},{7,4},{6,5},{4,7},{9,10},{11,8},{10,... | collective-permute-start | bytes 417800 | tf_op jit(solution)/shard_map/ppermute | solution.py:396
  147.4 8.4 %collective-permute-start.17 = (s16[17,32,128]{2,1,0:T(8,128)(2,1)S(1)}, s16[17,32,128]{2,1,0:T(8,128)(2,1)S(1)}, u32[]{:S(2)}, u32[]{:S(2)}) collective-permute-start(s16[17,32,128]{2,1,0:T(8,128)(2,1)S(1)} %get-tuple-element.62.refs_1_), channel_id=1, source_target_pairs={{0,1},{1,0},{2,3},{3,2},{4,5},{5,4},{6,7},{7,6},{8,9},{9,8},{10,11... | collective-permute-start | bytes 417800 | tf_op jit(solution)/shard_map/ppermute | solution.py:390
  150.7 6.8 %collective-permute-start.19 = (s16[17,32,128]{2,1,0:T(8,128)(2,1)S(1)}, s16[17,32,128]{2,1,0:T(8,128)(2,1)S(1)}, u32[]{:S(2)}, u32[]{:S(2)}) collective-permute-start(s16[17,32,128]{2,1,0:T(8,128)(2,1)S(1)} %get-tuple-element.61.refs_0_), channel_id=1, source_target_pairs={{0,1},{1,0},{2,3},{3,2},{4,5},{5,4},{6,7},{7,6},{8,9},{9,8},{10,11... | collective-permute-start | bytes 417800 | tf_op jit(solution)/shard_map/ppermute | solution.py:390
  150.8 7.3 %collective-permute-start.20 = (s16[17,32,128]{2,1,0:T(8,128)(2,1)S(1)}, s16[17,32,128]{2,1,0:T(8,128)(2,1)S(1)}, u32[]{:S(2)}, u32[]{:S(2)}) collective-permute-start(s16[17,32,128]{2,1,0:T(8,128)(2,1)S(1)} %get-tuple-element.62.refs_1_), channel_id=1, source_target_pairs={{1,2},{3,0},{2,1},{0,3},{5,6},{7,4},{6,5},{4,7},{9,10},{11,8},{10,... | collective-permute-start | bytes 417800 | tf_op jit(solution)/shard_map/ppermute | solution.py:396
  152.6 7.3 %collective-permute-start.16 = (s16[17,32,128]{2,1,0:T(8,128)(2,1)S(1)}, s16[17,32,128]{2,1,0:T(8,128)(2,1)S(1)}, u32[]{:S(2)}, u32[]{:S(2)}) collective-permute-start(s16[17,32,128]{2,1,0:T(8,128)(2,1)S(1)} %collective-permute-done.15.refs_4_), channel_id=1, source_target_pairs={{0,1},{1,0},{2,3},{3,2},{4,5},{5,4},{6,7},{7,6},{8,9},{9,8},{10,11... | collective-permute-start | bytes 417800 | tf_op jit(solution)/shard_map/ppermute | solution.py:390
  155.8 6.3 %collective-permute-start.18 = (s16[17,32,128]{2,1,0:T(8,128)(2,1)S(1)}, s16[17,32,128]{2,1,0:T(8,128)(2,1)S(1)}, u32[]{:S(2)}, u32[]{:S(2)}) collective-permute-start(s16[17,32,128]{2,1,0:T(8,128)(2,1)S(1)} %collective-permute-done.17.refs_3_), channel_id=1, source_target_pairs={{1,2},{3,0},{2,1},{0,3},{5,6},{7,4},{6,5},{4,7},{9,10},{11,8},{10,... | collective-permute-start | bytes 417800 | tf_op jit(solution)/shard_map/ppermute | solution.py:396
  (3 other events, 4.5 us)

commit v2 on v1

--- a/solution.py
+++ b/solution.py
@@ -263,7 +263,8 @@
     send_x(out, send_near, send_far)
 
 
-def gather_side_kernel(which, part, got, out, send_near, send_far):
+def gather_side_kernel(which, part, got, *refs):
+    out, send_near, send_far = refs[-3:]
     scale, side = scale_of(got), got.shape[1]
 
     def add(odd):
@@ -499,7 +500,7 @@
     side_shape = (shape(ext, side),) + (codes(side + 1, side),) * 2
     from_far, from_near = swap_far(send_far, "brick"), swap_near(send_near, "brick")
     total_near, nn, nf = call(partial(gather_side_kernel, 0), side_shape, [], 0, part, from_near)
-    total_far, fn, ff = call(partial(gather_side_kernel, 1), side_shape, [], 0, part, from_far)
+    total_far, fn, ff = call(partial(gather_side_kernel, 1), side_shape, [], 0, part, from_far, total_near)
     side = REACH
     kept, part, send_near, send_far = call(
         full_kernel,

time: 164 us -> 158 us (0.963)
  starting transfers between devices: 49.2 us -> 46.4 us
  waiting for transfers between devices: 69.2 us -> 66.6 us
    ppermute x10, starting transfers between devices: 15.1 us -> 12.5 us  [swap_near(): lax.ppermute(a, axis, [(i, i ^ 1) for i in range(lax.axis_size(axis))])]
    ppermute x10, waiting for transfers between devices: 19.3 us -> 17.3 us  [swap_far(): return lax.ppermute(a, axis, pairs + [(j, i) for i, j in pairs])]
  transfers between devices with their start and end apart: 22 -> 22, of which waited for: 8 -> 7; matrix products, arithmetic and copies ran while one was open for 3% -> 3% of each run, Pallas kernels for 7% -> 7%
where the time goes in v2:
time: 158 us
  waiting for transfers between devices  66.6 us (42%)
  starting transfers between devices  46.4 us (29%)
  Pallas kernels  34.2 us (22%)
  local copies, waits for them, and re-layouts  6.14 us (4%)
  other arithmetic  2.44 us (2%)
    all_to_all x1, waiting for transfers between devices, per_device(): got = lax.all_to_all(sending, BOTH, 0, 0, tiled=True)  41.4 us
    pallas_call x10, Pallas kernels, call(): pl.pallas_call(kernel, out_shape=out_shape, in_specs=[SMEM] * scalars + [...  33.3 us
    ppermute x10, starting transfers between devices, swap_far(): return lax.ppermute(a, axis, pairs + [(j, i) for i, j in pairs])  21.9 us
    ppermute x10, waiting for transfers between devices, swap_far(): return lax.ppermute(a, axis, pairs + [(j, i) for i, j in pairs])  17.3 us
    ppermute x10, starting transfers between devices, swap_near(): lax.ppermute(a, axis, [(i, i ^ 1) for i in range(lax.axis_size(axis))])  12.5 us
    all_to_all x1, starting transfers between devices, per_device(): got = lax.all_to_all(sending, BOTH, 0, 0, tiled=True)  10.6 us
    ppermute x10, waiting for transfers between devices, swap_near(): lax.ppermute(a, axis, [(i, i ^ 1) for i in range(lax.axis_size(axis))])  7.89 us
    unnamed x10, local copies, waits for them, and re-layouts  4.51 us
  transfers between devices with their start and end apart: 22, of which 7 were waited for; matrix products, arithmetic and copies ran while one was open for 3% of the time, Pallas kernels for 7%

profile of v2, /device:TPU:2, one launch (start us, length us, event | category | flops | bytes accessed | tf_op | source)
XLA Modules:
  0.0 157.7 jit_solution(13686941399200055110)
XLA Ops:
  0.0 1.6 %copy-done = f32[32,128,128]{2,1,0:T(8,128)S(1)} copy-done((f32[32,128,128]{2,1,0:T(8,128)S(1)}, f32[32,128,128]{2,1,0:T(8,128)}, u32[]{:S(2)}) %copy-start) | copy-done | bytes 2097176
  2.5 3.0 %collective-permute-start.3 = (f32[2,128]{1,0:T(2,128)S(1)}, f32[2,128]{1,0:T(2,128)S(1)}, u32[]{:S(2)}, u32[]{:S(2)}) collective-permute-start(f32[2,128]{1,0:T(2,128)S(1)} %select_maximum_fusion), channel_id=1, source_target_pairs={{1,2},{3,0},{2,1},{0,3},{5,6},{7,4},{6,5},{4,7},{9,10},{11,8},{10,... | collective-permute-start | bytes 3080 | tf_op jit(solution)/shard_map/ppermute | solution.py:397
  7.2 6.0 %collective-permute-start.1 = (bf16[64,16,128]{2,1,0:T(8,128)(2,1)S(1)}, bf16[64,16,128]{2,1,0:T(8,128)(2,1)S(1)}, u32[]{:S(2)}, u32[]{:S(2)}) collective-permute-start(bf16[64,16,128]{2,1,0:T(8,128)(2,1)S(1)} %get-tuple-element.37), channel_id=1, source_target_pairs={{4,8},{12,16},{20,24},{28,32},{36,40},{44,48},{52,56},{60,64},{68,... | collective-permute-start | bytes 786440 | tf_op jit(solution)/shard_map/ppermute | solution.py:397
  13.4 3.8 %shard_map.46 = bf16[32,4,2,2,32,128]{5,4,3,2,1,0:T(8,128)(2,1)} custom-call(bf16[2,32,2,128,128]{4,3,2,1,0:T(8,128)(2,1)} %bitcast.44), custom_call_target="tpu_custom_call" | custom-call | bytes 4194304 | tf_op jit(solution)/shard_map/pallas_call | solution.py:368
  17.4 10.6 %all-to-all-start = ((bf16[128,4,32,128]{3,2,1,0:T(8,128)(2,1)}), bf16[128,4,32,128]{3,2,1,0:T(8,128)(2,1)}, u32[]{:S(2)}, u32[]{:S(2)}) async-start(bf16[128,4,32,128]{3,2,1,0:T(8,128)(2,1)} %bitcast.43), calls=%async_computation | async-start | bytes 8388608 | tf_op jit(solution)/shard_map/all_to_all | solution.py:456
  32.6 4.5 %shard_map.48.blurred = bf16[8,1024,128]{2,1,0:T(8,128)(2,1)S(1)} custom-call(bf16[64,16,128]{2,1,0:T(8,128)(2,1)S(1)} %collective-permute-done.near, f32[64,32,128]{2,1,0:T(8,128)S(1)} %get-tuple-element.42.middle, bf16[64,16,128]{2,1,0:T(8,128)(2,1)S(1)} %collective-permute-done.1.far, bf16[256,128]{1,0:T(8,128)(2,1)S(1)} %pad_maximum_fusion.3.ax, ...), custom_call_target="tpu_custom_call" | custom-call | flops 4000000000 | bytes 2228224 | tf_op jit(solution)/shard_map/pallas_call | solution.py:368
  38.5 41.4 %all-to-all-done = bf16[128,4,32,128]{3,2,1,0:T(8,128)(2,1)} async-done(((bf16[128,4,32,128]{3,2,1,0:T(8,128)(2,1)}), bf16[128,4,32,128]{3,2,1,0:T(8,128)(2,1)}, u32[]{:S(2)}, u32[]{:S(2)}) %all-to-all-start) | async-done | bytes 4194336 | tf_op jit(solution)/shard_map/all_to_all | solution.py:456
  79.9 1.6 %copy-done.2 = bf16[8,1024,128]{2,1,0:T(8,128)(2,1)S(1)} copy-done((bf16[8,1024,128]{2,1,0:T(8,128)(2,1)S(1)}, bf16[8,1024,128]{2,1,0:T(8,128)(2,1)}, u32[]{:S(2)}) %copy-start.2) | copy-done | bytes 2097176
  81.5 7.9 %shard_map.49 = (f32[64,64,128]{2,1,0:T(8,128)S(1)}, s16[65,32,128]{2,1,0:T(8,128)(2,1)S(1)}, s16[65,32,128]{2,1,0:T(8,128)(2,1)S(1)}) custom-call(s32[256]{0:T(256)S(1)} %reshape.94.where, bf16[8,1024,128]{2,1,0:T(8,128)(2,1)S(1)} %copy-done.2, bf16[512,32,128]{2,1,0:T(8,128)(2,1)} %bitcast.21.got, bf16[128,256]{1,0:T(8,128)(2,1)S(1)} %pad_maximum_fusion.5.axt, ...), custom_call_target="tpu_custom_call" | custom-call | flops 4000000000 | bytes 6947840 | tf_op jit(solution)/shard_map/pallas_call | solution.py:368
  89.8 2.9 %collective-permute-start.6 = (s16[65,32,128]{2,1,0:T(8,128)(2,1)S(1)}, s16[65,32,128]{2,1,0:T(8,128)(2,1)S(1)}, u32[]{:S(2)}, u32[]{:S(2)}) collective-permute-start(s16[65,32,128]{2,1,0:T(8,128)(2,1)S(1)} %get-tuple-element.48), channel_id=1, source_target_pairs={{4,8},{12,16},{20,24},{28,32},{36,40},{44,48},{52,56},{60,64},{68,... | collective-permute-start | bytes 1597448 | tf_op jit(solution)/shard_map/ppermute | solution.py:397
  95.0 7.5 %collective-permute-done.6.got = s16[65,32,128]{2,1,0:T(8,128)(2,1)S(1)} collective-permute-done((s16[65,32,128]{2,1,0:T(8,128)(2,1)S(1)}, s16[65,32,128]{2,1,0:T(8,128)(2,1)S(1)}, u32[]{:S(2)}, u32[]{:S(2)}) %collective-permute-start.6) | collective-permute-done | bytes 532512 | tf_op jit(solution)/shard_map/ppermute | solution.py:397
  104.6 5.5 %collective-permute-done.9.got_fn = s16[33,32,128]{2,1,0:T(8,128)(2,1)S(1)} collective-permute-done((s16[33,32,128]{2,1,0:T(8,128)(2,1)S(1)}, s16[33,32,128]{2,1,0:T(8,128)(2,1)S(1)}, u32[]{:S(2)}, u32[]{:S(2)}) %collective-permute-start.9) | collective-permute-done | bytes 270368 | tf_op jit(solution)/shard_map/ppermute | solution.py:391
  110.1 12.3 %shard_map.52 = (f32[64,32,128]{2,1,0:T(8,128)S(1)}, f32[64,64,128]{2,1,0:T(8,128)S(1)}, s16[65,16,128]{2,1,0:T(8,128)(2,1)S(1)}, s16[65,16,128]{2,1,0:T(8,128)(2,1)S(1)}) custom-call(s32[256]{0:T(256)S(1)} %reshape.94.where, bf16[64,16,128]{2,1,0:T(8,128)(2,1)S(1)} %collective-permute-done.near, f32[64,32,128]{2,1,0:T(8,128)S(1)} %get-tuple-element.42.middle, ...), custom_call_target="tpu_custom_call" | custom-call | flops 8000000000 | bytes 10257408 | tf_op jit(solution)/shard_map/pallas_call | solution.py:368
  122.5 3.0 %collective-permute-start.12 = (s16[65,16,128]{2,1,0:T(8,128)(2,1)S(1)}, s16[65,16,128]{2,1,0:T(8,128)(2,1)S(1)}, u32[]{:S(2)}, u32[]{:S(2)}) collective-permute-start(s16[65,16,128]{2,1,0:T(8,128)(2,1)S(1)} %get-tuple-element.57), channel_id=1, source_target_pairs={{4,8},{12,16},{20,24},{28,32},{36,40},{44,48},{52,56},{60,64},{68,... | collective-permute-start | bytes 798728 | tf_op jit(solution)/shard_map/ppermute | solution.py:397
  125.5 6.9 %collective-permute-done.12.far = s16[65,16,128]{2,1,0:T(8,128)(2,1)S(1)} collective-permute-done((s16[65,16,128]{2,1,0:T(8,128)(2,1)S(1)}, s16[65,16,128]{2,1,0:T(8,128)(2,1)S(1)}, u32[]{:S(2)}, u32[]{:S(2)}) %collective-permute-start.12) | collective-permute-done | bytes 266272 | tf_op jit(solution)/shard_map/ppermute | solution.py:397
  133.1 3.7 %collective-permute-start.13 = (s16[17,32,128]{2,1,0:T(8,128)(2,1)S(1)}, s16[17,32,128]{2,1,0:T(8,128)(2,1)S(1)}, u32[]{:S(2)}, u32[]{:S(2)}) collective-permute-start(s16[17,32,128]{2,1,0:T(8,128)(2,1)S(1)} %get-tuple-element.59), channel_id=1, source_target_pairs={{0,1},{1,0},{2,3},{3,2},{4,5},{5,4},{6,7},{7,6},{8,9},{9,8},{10,11... | collective-permute-start | bytes 417800 | tf_op jit(solution)/shard_map/ppermute | solution.py:391
  137.4 2.4 %collective-permute-done.13.near = s16[17,32,128]{2,1,0:T(8,128)(2,1)S(1)} collective-permute-done((s16[17,32,128]{2,1,0:T(8,128)(2,1)S(1)}, s16[17,32,128]{2,1,0:T(8,128)(2,1)S(1)}, u32[]{:S(2)}, u32[]{:S(2)}) %collective-permute-start.13) | collective-permute-done | bytes 139296 | tf_op jit(solution)/shard_map/ppermute | solution.py:391
  140.3 1.7 %collective-permute-start.15 = (s16[17,32,128]{2,1,0:T(8,128)(2,1)S(1)}, s16[17,32,128]{2,1,0:T(8,128)(2,1)S(1)}, u32[]{:S(2)}, u32[]{:S(2)}) collective-permute-start(s16[17,32,128]{2,1,0:T(8,128)(2,1)S(1)} %get-tuple-element.61.refs_0_), channel_id=1, source_target_pairs={{1,2},{3,0},{2,1},{0,3},{5,6},{7,4},{6,5},{4,7},{9,10},{11,8},{10,... | collective-permute-start | bytes 417800 | tf_op jit(solution)/shard_map/ppermute | solution.py:397
  142.0 3.3 %collective-permute-start.17 = (s16[17,32,128]{2,1,0:T(8,128)(2,1)S(1)}, s16[17,32,128]{2,1,0:T(8,128)(2,1)S(1)}, u32[]{:S(2)}, u32[]{:S(2)}) collective-permute-start(s16[17,32,128]{2,1,0:T(8,128)(2,1)S(1)} %get-tuple-element.62.refs_1_), channel_id=1, source_target_pairs={{0,1},{1,0},{2,3},{3,2},{4,5},{5,4},{6,7},{7,6},{8,9},{9,8},{10,11... | collective-permute-start | bytes 417800 | tf_op jit(solution)/shard_map/ppermute | solution.py:391
  145.4 1.6 %collective-permute-start.20 = (s16[17,32,128]{2,1,0:T(8,128)(2,1)S(1)}, s16[17,32,128]{2,1,0:T(8,128)(2,1)S(1)}, u32[]{:S(2)}, u32[]{:S(2)}) collective-permute-start(s16[17,32,128]{2,1,0:T(8,128)(2,1)S(1)} %get-tuple-element.62.refs_1_), channel_id=1, source_target_pairs={{1,2},{3,0},{2,1},{0,3},{5,6},{7,4},{6,5},{4,7},{9,10},{11,8},{10,... | collective-permute-start | bytes 417800 | tf_op jit(solution)/shard_map/ppermute | solution.py:397
  147.0 3.4 %collective-permute-start.16 = (s16[17,32,128]{2,1,0:T(8,128)(2,1)S(1)}, s16[17,32,128]{2,1,0:T(8,128)(2,1)S(1)}, u32[]{:S(2)}, u32[]{:S(2)}) collective-permute-start(s16[17,32,128]{2,1,0:T(8,128)(2,1)S(1)} %collective-permute-done.15.refs_4_), channel_id=1, source_target_pairs={{0,1},{1,0},{2,3},{3,2},{4,5},{5,4},{6,7},{7,6},{8,9},{9,8},{10,11... | collective-permute-start | bytes 417800 | tf_op jit(solution)/shard_map/ppermute | solution.py:391
  150.4 1.6 %collective-permute-start.18 = (s16[17,32,128]{2,1,0:T(8,128)(2,1)S(1)}, s16[17,32,128]{2,1,0:T(8,128)(2,1)S(1)}, u32[]{:S(2)}, u32[]{:S(2)}) collective-permute-start(s16[17,32,128]{2,1,0:T(8,128)(2,1)S(1)} %collective-permute-done.17.refs_3_), channel_id=1, source_target_pairs={{1,2},{3,0},{2,1},{0,3},{5,6},{7,4},{6,5},{4,7},{9,10},{11,8},{10,... | collective-permute-start | bytes 417800 | tf_op jit(solution)/shard_map/ppermute | solution.py:397
  152.5 1.8 %shard_map.55._ = f32[32,128,128]{2,1,0:T(8,128)} custom-call(s16[17,32,128]{2,1,0:T(8,128)(2,1)S(1)} %get-tuple-element.61.refs_0_, s16[17,32,128]{2,1,0:T(8,128)(2,1)S(1)} %get-tuple-element.62.refs_1_, s16[17,32,128]{2,1,0:T(8,128)(2,1)S(1)} %collective-permute-done.19.refs_2_, s16[17,32,128]{2,1,0:T(8,128)(2,1)S(1)} %collective-permute-done.17.refs_3_, ...), custom_call_target="tpu_custom_call" | custom-call | bytes 835584 | tf_op jit(solution)/shard_map/pallas_call | solution.py:368
  154.3 2.3 %collective-permute-done.18.upper = s16[17,32,128]{2,1,0:T(8,128)(2,1)S(1)} collective-permute-done((s16[17,32,128]{2,1,0:T(8,128)(2,1)S(1)}, s16[17,32,128]{2,1,0:T(8,128)(2,1)S(1)}, u32[]{:S(2)}, u32[]{:S(2)}) %collective-permute-start.18) | collective-permute-done | bytes 139296 | tf_op jit(solution)/shard_map/ppermute | solution.py:397
  (84 shorter events, 16.8 us)
Async XLA Ops:
  0.0 2.2 %copy-start.4 = (s32[2,1024,1]{1,2,0:T(1,128)S(1)}, s32[2,1024,1]{1,2,0:T(1,128)}, u32[]{:S(2)}) copy-start(s32[2,1024,1]{1,2,0:T(1,128)} %param.7) | copy-start | bytes 24580
  0.0 1.9 %copy-start.3 = (f32[2,3,31]{2,0,1:T(2,128)S(1)}, f32[2,3,31]{2,0,1:T(2,128)}, u32[]{:S(2)}) copy-start(f32[2,3,31]{2,0,1:T(2,128)} %param.6) | copy-start | bytes 2236
  2.5 14.7 %collective-permute-start.3 = (f32[2,128]{1,0:T(2,128)S(1)}, f32[2,128]{1,0:T(2,128)S(1)}, u32[]{:S(2)}, u32[]{:S(2)}) collective-permute-start(f32[2,128]{1,0:T(2,128)S(1)} %select_maximum_fusion), channel_id=1, source_target_pairs={{1,2},{3,0},{2,1},{0,3},{5,6},{7,4},{6,5},{4,7},{9,10},{11,8},{10,... | collective-permute-start | bytes 3080 | tf_op jit(solution)/shard_map/ppermute | solution.py:397
  5.5 11.7 %collective-permute-start.2 = (f32[2,128]{1,0:T(2,128)S(1)}, f32[2,128]{1,0:T(2,128)S(1)}, u32[]{:S(2)}, u32[]{:S(2)}) collective-permute-start(f32[2,128]{1,0:T(2,128)S(1)} %select_maximum_fusion), channel_id=1, source_target_pairs={{0,1},{1,0},{2,3},{3,2},{4,5},{5,4},{6,7},{7,6},{8,9},{9,8},{10,11... | collective-permute-start | bytes 3080 | tf_op jit(solution)/shard_map/ppermute | solution.py:391
  5.7 11.6 %collective-permute-start.4 = (f32[2,128]{1,0:T(2,128)S(1)}, f32[2,128]{1,0:T(2,128)S(1)}, u32[]{:S(2)}, u32[]{:S(2)}) collective-permute-start(f32[2,128]{1,0:T(2,128)S(1)} %select_maximum_fusion), channel_id=1, source_target_pairs={{0,2},{1,3},{2,0},{3,1},{4,6},{5,7},{6,4},{7,5},{8,10},{9,11},{10,... | collective-permute-start | bytes 3080 | tf_op jit(solution)/shard_map/ppermute | solution.py:435
  7.2 10.1 %collective-permute-start = (bf16[64,16,128]{2,1,0:T(8,128)(2,1)S(1)}, bf16[64,16,128]{2,1,0:T(8,128)(2,1)S(1)}, u32[]{:S(2)}, u32[]{:S(2)}) collective-permute-start(bf16[64,16,128]{2,1,0:T(8,128)(2,1)S(1)} %get-tuple-element.36), channel_id=1, source_target_pairs={{0,4},{4,0},{8,12},{12,8},{16,20},{20,16},{24,28},{28,24},{32,36},... | collective-permute-start | bytes 786440 | tf_op jit(solution)/shard_map/ppermute | solution.py:391
  7.2 10.1 %collective-permute-start.1 = (bf16[64,16,128]{2,1,0:T(8,128)(2,1)S(1)}, bf16[64,16,128]{2,1,0:T(8,128)(2,1)S(1)}, u32[]{:S(2)}, u32[]{:S(2)}) collective-permute-start(bf16[64,16,128]{2,1,0:T(8,128)(2,1)S(1)} %get-tuple-element.37), channel_id=1, source_target_pairs={{4,8},{12,16},{20,24},{28,32},{36,40},{44,48},{52,56},{60,64},{68,... | collective-permute-start | bytes 786440 | tf_op jit(solution)/shard_map/ppermute | solution.py:397
  17.4 62.5 %all-to-all-start = ((bf16[128,4,32,128]{3,2,1,0:T(8,128)(2,1)}), bf16[128,4,32,128]{3,2,1,0:T(8,128)(2,1)}, u32[]{:S(2)}, u32[]{:S(2)}) async-start(bf16[128,4,32,128]{3,2,1,0:T(8,128)(2,1)} %bitcast.43), calls=%async_computation | async-start | bytes 8388608 | tf_op jit(solution)/shard_map/all_to_all | solution.py:456
  89.4 3.4 %collective-permute-start.5 = (s16[65,32,128]{2,1,0:T(8,128)(2,1)S(1)}, s16[65,32,128]{2,1,0:T(8,128)(2,1)S(1)}, u32[]{:S(2)}, u32[]{:S(2)}) collective-permute-start(s16[65,32,128]{2,1,0:T(8,128)(2,1)S(1)} %get-tuple-element.46), channel_id=1, source_target_pairs={{0,4},{4,0},{8,12},{12,8},{16,20},{20,16},{24,28},{28,24},{32,36},... | collective-permute-start | bytes 1597448 | tf_op jit(solution)/shard_map/ppermute | solution.py:391
  89.8 12.7 %collective-permute-start.6 = (s16[65,32,128]{2,1,0:T(8,128)(2,1)S(1)}, s16[65,32,128]{2,1,0:T(8,128)(2,1)S(1)}, u32[]{:S(2)}, u32[]{:S(2)}) collective-permute-start(s16[65,32,128]{2,1,0:T(8,128)(2,1)S(1)} %get-tuple-element.48), channel_id=1, source_target_pairs={{4,8},{12,16},{20,24},{28,32},{36,40},{44,48},{52,56},{60,64},{68,... | collective-permute-start | bytes 1597448 | tf_op jit(solution)/shard_map/ppermute | solution.py:397
  93.6 11.0 %collective-permute-start.7 = (s16[33,32,128]{2,1,0:T(8,128)(2,1)S(1)}, s16[33,32,128]{2,1,0:T(8,128)(2,1)S(1)}, u32[]{:S(2)}, u32[]{:S(2)}) collective-permute-start(s16[33,32,128]{2,1,0:T(8,128)(2,1)S(1)} %get-tuple-element.50), channel_id=1, source_target_pairs={{0,1},{1,0},{2,3},{3,2},{4,5},{5,4},{6,7},{7,6},{8,9},{9,8},{10,11... | collective-permute-start | bytes 811016 | tf_op jit(solution)/shard_map/ppermute | solution.py:391
  94.3 10.3 %collective-permute-start.8 = (s16[33,32,128]{2,1,0:T(8,128)(2,1)S(1)}, s16[33,32,128]{2,1,0:T(8,128)(2,1)S(1)}, u32[]{:S(2)}, u32[]{:S(2)}) collective-permute-start(s16[33,32,128]{2,1,0:T(8,128)(2,1)S(1)} %get-tuple-element.51), channel_id=1, source_target_pairs={{1,2},{2,1},{5,6},{6,5},{9,10},{10,9},{13,14},{14,13},{17,18},{18,... | collective-permute-start | bytes 811016 | tf_op jit(solution)/shard_map/ppermute | solution.py:397
  103.3 6.8 %collective-permute-start.9 = (s16[33,32,128]{2,1,0:T(8,128)(2,1)S(1)}, s16[33,32,128]{2,1,0:T(8,128)(2,1)S(1)}, u32[]{:S(2)}, u32[]{:S(2)}) collective-permute-start(s16[33,32,128]{2,1,0:T(8,128)(2,1)S(1)} %get-tuple-element.52), channel_id=1, source_target_pairs={{0,1},{1,0},{2,3},{3,2},{4,5},{5,4},{6,7},{7,6},{8,9},{9,8},{10,11... | collective-permute-start | bytes 811016 | tf_op jit(solution)/shard_map/ppermute | solution.py:391
  103.9 6.2 %collective-permute-start.10 = (s16[33,32,128]{2,1,0:T(8,128)(2,1)S(1)}, s16[33,32,128]{2,1,0:T(8,128)(2,1)S(1)}, u32[]{:S(2)}, u32[]{:S(2)}) collective-permute-start(s16[33,32,128]{2,1,0:T(8,128)(2,1)S(1)} %get-tuple-element.53), channel_id=1, source_target_pairs={{1,2},{2,1},{5,6},{6,5},{9,10},{10,9},{13,14},{14,13},{17,18},{18,... | collective-permute-start | bytes 811016 | tf_op jit(solution)/shard_map/ppermute | solution.py:397
  122.4 3.1 %collective-permute-start.11 = (s16[65,16,128]{2,1,0:T(8,128)(2,1)S(1)}, s16[65,16,128]{2,1,0:T(8,128)(2,1)S(1)}, u32[]{:S(2)}, u32[]{:S(2)}) collective-permute-start(s16[65,16,128]{2,1,0:T(8,128)(2,1)S(1)} %get-tuple-element.56), channel_id=1, source_target_pairs={{0,4},{4,0},{8,12},{12,8},{16,20},{20,16},{24,28},{28,24},{32,36},... | collective-permute-start | bytes 798728 | tf_op jit(solution)/shard_map/ppermute | solution.py:391
  122.5 9.8 %collective-permute-start.12 = (s16[65,16,128]{2,1,0:T(8,128)(2,1)S(1)}, s16[65,16,128]{2,1,0:T(8,128)(2,1)S(1)}, u32[]{:S(2)}, u32[]{:S(2)}) collective-permute-start(s16[65,16,128]{2,1,0:T(8,128)(2,1)S(1)} %get-tuple-element.57), channel_id=1, source_target_pairs={{4,8},{12,16},{20,24},{28,32},{36,40},{44,48},{52,56},{60,64},{68,... | collective-permute-start | bytes 798728 | tf_op jit(solution)/shard_map/ppermute | solution.py:397
  133.1 6.8 %collective-permute-start.13 = (s16[17,32,128]{2,1,0:T(8,128)(2,1)S(1)}, s16[17,32,128]{2,1,0:T(8,128)(2,1)S(1)}, u32[]{:S(2)}, u32[]{:S(2)}) collective-permute-start(s16[17,32,128]{2,1,0:T(8,128)(2,1)S(1)} %get-tuple-element.59), channel_id=1, source_target_pairs={{0,1},{1,0},{2,3},{3,2},{4,5},{5,4},{6,7},{7,6},{8,9},{9,8},{10,11... | collective-permute-start | bytes 417800 | tf_op jit(solution)/shard_map/ppermute | solution.py:391
  136.8 3.0 %collective-permute-start.14 = (s16[17,32,128]{2,1,0:T(8,128)(2,1)S(1)}, s16[17,32,128]{2,1,0:T(8,128)(2,1)S(1)}, u32[]{:S(2)}, u32[]{:S(2)}) collective-permute-start(s16[17,32,128]{2,1,0:T(8,128)(2,1)S(1)} %get-tuple-element.60), channel_id=1, source_target_pairs={{1,2},{2,1},{5,6},{6,5},{9,10},{10,9},{13,14},{14,13},{17,18},{18,... | collective-permute-start | bytes 417800 | tf_op jit(solution)/shard_map/ppermute | solution.py:397
  140.3 6.7 %collective-permute-start.15 = (s16[17,32,128]{2,1,0:T(8,128)(2,1)S(1)}, s16[17,32,128]{2,1,0:T(8,128)(2,1)S(1)}, u32[]{:S(2)}, u32[]{:S(2)}) collective-permute-start(s16[17,32,128]{2,1,0:T(8,128)(2,1)S(1)} %get-tuple-element.61.refs_0_), channel_id=1, source_target_pairs={{1,2},{3,0},{2,1},{0,3},{5,6},{7,4},{6,5},{4,7},{9,10},{11,8},{10,... | collective-permute-start | bytes 417800 | tf_op jit(solution)/shard_map/ppermute | solution.py:397
  142.0 8.4 %collective-permute-start.17 = (s16[17,32,128]{2,1,0:T(8,128)(2,1)S(1)}, s16[17,32,128]{2,1,0:T(8,128)(2,1)S(1)}, u32[]{:S(2)}, u32[]{:S(2)}) collective-permute-start(s16[17,32,128]{2,1,0:T(8,128)(2,1)S(1)} %get-tuple-element.62.refs_1_), channel_id=1, source_target_pairs={{0,1},{1,0},{2,3},{3,2},{4,5},{5,4},{6,7},{7,6},{8,9},{9,8},{10,11... | collective-permute-start | bytes 417800 | tf_op jit(solution)/shard_map/ppermute | solution.py:391
  145.3 6.7 %collective-permute-start.19 = (s16[17,32,128]{2,1,0:T(8,128)(2,1)S(1)}, s16[17,32,128]{2,1,0:T(8,128)(2,1)S(1)}, u32[]{:S(2)}, u32[]{:S(2)}) collective-permute-start(s16[17,32,128]{2,1,0:T(8,128)(2,1)S(1)} %get-tuple-element.61.refs_0_), channel_id=1, source_target_pairs={{0,1},{1,0},{2,3},{3,2},{4,5},{5,4},{6,7},{7,6},{8,9},{9,8},{10,11... | collective-permute-start | bytes 417800 | tf_op jit(solution)/shard_map/ppermute | solution.py:391
  145.4 7.2 %collective-permute-start.20 = (s16[17,32,128]{2,1,0:T(8,128)(2,1)S(1)}, s16[17,32,128]{2,1,0:T(8,128)(2,1)S(1)}, u32[]{:S(2)}, u32[]{:S(2)}) collective-permute-start(s16[17,32,128]{2,1,0:T(8,128)(2,1)S(1)} %get-tuple-element.62.refs_1_), channel_id=1, source_target_pairs={{1,2},{3,0},{2,1},{0,3},{5,6},{7,4},{6,5},{4,7},{9,10},{11,8},{10,... | collective-permute-start | bytes 417800 | tf_op jit(solution)/shard_map/ppermute | solution.py:397
  147.0 7.4 %collective-permute-start.16 = (s16[17,32,128]{2,1,0:T(8,128)(2,1)S(1)}, s16[17,32,128]{2,1,0:T(8,128)(2,1)S(1)}, u32[]{:S(2)}, u32[]{:S(2)}) collective-permute-start(s16[17,32,128]{2,1,0:T(8,128)(2,1)S(1)} %collective-permute-done.15.refs_4_), channel_id=1, source_target_pairs={{0,1},{1,0},{2,3},{3,2},{4,5},{5,4},{6,7},{7,6},{8,9},{9,8},{10,11... | collective-permute-start | bytes 417800 | tf_op jit(solution)/shard_map/ppermute | solution.py:391
  150.4 6.3 %collective-permute-start.18 = (s16[17,32,128]{2,1,0:T(8,128)(2,1)S(1)}, s16[17,32,128]{2,1,0:T(8,128)(2,1)S(1)}, u32[]{:S(2)}, u32[]{:S(2)}) collective-permute-start(s16[17,32,128]{2,1,0:T(8,128)(2,1)S(1)} %collective-permute-done.17.refs_3_), channel_id=1, source_target_pairs={{1,2},{3,0},{2,1},{0,3},{5,6},{7,4},{6,5},{4,7},{9,10},{11,8},{10,... | collective-permute-start | bytes 417800 | tf_op jit(solution)/shard_map/ppermute | solution.py:397
  (3 other events, 4.5 us)

commit v3 on v2

--- a/solution.py
+++ b/solution.py
@@ -117,7 +117,7 @@
         body(pl.multiple_of(n * 8, 8))
         return carry
 
-    lax.fori_loop(0, count // 8, step, 0)
+    lax.fori_loop(0, count // 8, step, 0, unroll=True)
 
 
 def send_part(part, *messages):

time: 158 us -> 158 us (level)
  no operation moved by 1% of the time
where the time goes in v3:
time: 158 us
  waiting for transfers between devices  66.6 us (42%)
  starting transfers between devices  46.4 us (29%)
  Pallas kernels  34.1 us (22%)
  local copies, waits for them, and re-layouts  6.14 us (4%)
  other arithmetic  2.44 us (2%)
    all_to_all x1, waiting for transfers between devices, per_device(): got = lax.all_to_all(sending, BOTH, 0, 0, tiled=True)  41.4 us
    pallas_call x10, Pallas kernels, call(): pl.pallas_call(kernel, out_shape=out_shape, in_specs=[SMEM] * scalars + [...  33.2 us
    ppermute x10, starting transfers between devices, swap_far(): return lax.ppermute(a, axis, pairs + [(j, i) for i, j in pairs])  21.9 us
    ppermute x10, waiting for transfers between devices, swap_far(): return lax.ppermute(a, axis, pairs + [(j, i) for i, j in pairs])  17.3 us
    ppermute x10, starting transfers between devices, swap_near(): lax.ppermute(a, axis, [(i, i ^ 1) for i in range(lax.axis_size(axis))])  12.5 us
    all_to_all x1, starting transfers between devices, per_device(): got = lax.all_to_all(sending, BOTH, 0, 0, tiled=True)  10.6 us
    ppermute x10, waiting for transfers between devices, swap_near(): lax.ppermute(a, axis, [(i, i ^ 1) for i in range(lax.axis_size(axis))])  7.89 us
    unnamed x10, local copies, waits for them, and re-layouts  4.51 us
  transfers between devices with their start and end apart: 22, of which 7 were waited for; matrix products, arithmetic and copies ran while one was open for 3% of the time, Pallas kernels for 7%

profile of v3, /device:TPU:2, one launch (start us, length us, event | category | flops | bytes accessed | tf_op | source)
XLA Modules:
  0.0 157.7 jit_solution(1861655076476987730)
XLA Ops:
  0.0 1.6 %copy-done = f32[32,128,128]{2,1,0:T(8,128)S(1)} copy-done((f32[32,128,128]{2,1,0:T(8,128)S(1)}, f32[32,128,128]{2,1,0:T(8,128)}, u32[]{:S(2)}) %copy-start) | copy-done | bytes 2097176
  2.5 3.0 %collective-permute-start.3 = (f32[2,128]{1,0:T(2,128)S(1)}, f32[2,128]{1,0:T(2,128)S(1)}, u32[]{:S(2)}, u32[]{:S(2)}) collective-permute-start(f32[2,128]{1,0:T(2,128)S(1)} %select_maximum_fusion), channel_id=1, source_target_pairs={{1,2},{3,0},{2,1},{0,3},{5,6},{7,4},{6,5},{4,7},{9,10},{11,8},{10,... | collective-permute-start | bytes 3080 | tf_op jit(solution)/shard_map/ppermute | solution.py:397
  7.2 6.0 %collective-permute-start.1 = (bf16[64,16,128]{2,1,0:T(8,128)(2,1)S(1)}, bf16[64,16,128]{2,1,0:T(8,128)(2,1)S(1)}, u32[]{:S(2)}, u32[]{:S(2)}) collective-permute-start(bf16[64,16,128]{2,1,0:T(8,128)(2,1)S(1)} %get-tuple-element.37), channel_id=1, source_target_pairs={{4,8},{12,16},{20,24},{28,32},{36,40},{44,48},{52,56},{60,64},{68,... | collective-permute-start | bytes 786440 | tf_op jit(solution)/shard_map/ppermute | solution.py:397
  13.4 3.8 %shard_map.46 = bf16[32,4,2,2,32,128]{5,4,3,2,1,0:T(8,128)(2,1)} custom-call(bf16[2,32,2,128,128]{4,3,2,1,0:T(8,128)(2,1)} %bitcast.44), custom_call_target="tpu_custom_call" | custom-call | bytes 4194304 | tf_op jit(solution)/shard_map/pallas_call | solution.py:368
  17.4 10.6 %all-to-all-start = ((bf16[128,4,32,128]{3,2,1,0:T(8,128)(2,1)}), bf16[128,4,32,128]{3,2,1,0:T(8,128)(2,1)}, u32[]{:S(2)}, u32[]{:S(2)}) async-start(bf16[128,4,32,128]{3,2,1,0:T(8,128)(2,1)} %bitcast.43), calls=%async_computation | async-start | bytes 8388608 | tf_op jit(solution)/shard_map/all_to_all | solution.py:456
  32.6 4.5 %shard_map.48.blurred = bf16[8,1024,128]{2,1,0:T(8,128)(2,1)S(1)} custom-call(bf16[64,16,128]{2,1,0:T(8,128)(2,1)S(1)} %collective-permute-done.near, f32[64,32,128]{2,1,0:T(8,128)S(1)} %get-tuple-element.42.middle, bf16[64,16,128]{2,1,0:T(8,128)(2,1)S(1)} %collective-permute-done.1.far, bf16[256,128]{1,0:T(8,128)(2,1)S(1)} %pad_maximum_fusion.3.ax, ...), custom_call_target="tpu_custom_call" | custom-call | flops 4000000000 | bytes 2228224 | tf_op jit(solution)/shard_map/pallas_call | solution.py:368
  38.5 41.4 %all-to-all-done = bf16[128,4,32,128]{3,2,1,0:T(8,128)(2,1)} async-done(((bf16[128,4,32,128]{3,2,1,0:T(8,128)(2,1)}), bf16[128,4,32,128]{3,2,1,0:T(8,128)(2,1)}, u32[]{:S(2)}, u32[]{:S(2)}) %all-to-all-start) | async-done | bytes 4194336 | tf_op jit(solution)/shard_map/all_to_all | solution.py:456
  79.9 1.6 %copy-done.2 = bf16[8,1024,128]{2,1,0:T(8,128)(2,1)S(1)} copy-done((bf16[8,1024,128]{2,1,0:T(8,128)(2,1)S(1)}, bf16[8,1024,128]{2,1,0:T(8,128)(2,1)}, u32[]{:S(2)}) %copy-start.2) | copy-done | bytes 2097176
  81.5 7.8 %shard_map.49 = (f32[64,64,128]{2,1,0:T(8,128)S(1)}, s16[65,32,128]{2,1,0:T(8,128)(2,1)S(1)}, s16[65,32,128]{2,1,0:T(8,128)(2,1)S(1)}) custom-call(s32[256]{0:T(256)S(1)} %reshape.94.where, bf16[8,1024,128]{2,1,0:T(8,128)(2,1)S(1)} %copy-done.2, bf16[512,32,128]{2,1,0:T(8,128)(2,1)} %bitcast.21.got, bf16[128,256]{1,0:T(8,128)(2,1)S(1)} %pad_maximum_fusion.5.axt, ...), custom_call_target="tpu_custom_call" | custom-call | flops 4000000000 | bytes 6947840 | tf_op jit(solution)/shard_map/pallas_call | solution.py:368
  89.8 2.9 %collective-permute-start.6 = (s16[65,32,128]{2,1,0:T(8,128)(2,1)S(1)}, s16[65,32,128]{2,1,0:T(8,128)(2,1)S(1)}, u32[]{:S(2)}, u32[]{:S(2)}) collective-permute-start(s16[65,32,128]{2,1,0:T(8,128)(2,1)S(1)} %get-tuple-element.48), channel_id=1, source_target_pairs={{4,8},{12,16},{20,24},{28,32},{36,40},{44,48},{52,56},{60,64},{68,... | collective-permute-start | bytes 1597448 | tf_op jit(solution)/shard_map/ppermute | solution.py:397
  94.8 7.6 %collective-permute-done.6.got = s16[65,32,128]{2,1,0:T(8,128)(2,1)S(1)} collective-permute-done((s16[65,32,128]{2,1,0:T(8,128)(2,1)S(1)}, s16[65,32,128]{2,1,0:T(8,128)(2,1)S(1)}, u32[]{:S(2)}, u32[]{:S(2)}) %collective-permute-start.6) | collective-permute-done | bytes 532512 | tf_op jit(solution)/shard_map/ppermute | solution.py:397
  104.7 5.5 %collective-permute-done.9.got_fn = s16[33,32,128]{2,1,0:T(8,128)(2,1)S(1)} collective-permute-done((s16[33,32,128]{2,1,0:T(8,128)(2,1)S(1)}, s16[33,32,128]{2,1,0:T(8,128)(2,1)S(1)}, u32[]{:S(2)}, u32[]{:S(2)}) %collective-permute-start.9) | collective-permute-done | bytes 270368 | tf_op jit(solution)/shard_map/ppermute | solution.py:391
  110.2 12.0 %shard_map.52 = (f32[64,32,128]{2,1,0:T(8,128)S(1)}, f32[64,64,128]{2,1,0:T(8,128)S(1)}, s16[65,16,128]{2,1,0:T(8,128)(2,1)S(1)}, s16[65,16,128]{2,1,0:T(8,128)(2,1)S(1)}) custom-call(s32[256]{0:T(256)S(1)} %reshape.94.where, bf16[64,16,128]{2,1,0:T(8,128)(2,1)S(1)} %collective-permute-done.near, f32[64,32,128]{2,1,0:T(8,128)S(1)} %get-tuple-element.42.middle, ...), custom_call_target="tpu_custom_call" | custom-call | flops 8000000000 | bytes 10257408 | tf_op jit(solution)/shard_map/pallas_call | solution.py:368
  122.3 3.0 %collective-permute-start.12 = (s16[65,16,128]{2,1,0:T(8,128)(2,1)S(1)}, s16[65,16,128]{2,1,0:T(8,128)(2,1)S(1)}, u32[]{:S(2)}, u32[]{:S(2)}) collective-permute-start(s16[65,16,128]{2,1,0:T(8,128)(2,1)S(1)} %get-tuple-element.57), channel_id=1, source_target_pairs={{4,8},{12,16},{20,24},{28,32},{36,40},{44,48},{52,56},{60,64},{68,... | collective-permute-start | bytes 798728 | tf_op jit(solution)/shard_map/ppermute | solution.py:397
  125.3 6.8 %collective-permute-done.12.far = s16[65,16,128]{2,1,0:T(8,128)(2,1)S(1)} collective-permute-done((s16[65,16,128]{2,1,0:T(8,128)(2,1)S(1)}, s16[65,16,128]{2,1,0:T(8,128)(2,1)S(1)}, u32[]{:S(2)}, u32[]{:S(2)}) %collective-permute-start.12) | collective-permute-done | bytes 266272 | tf_op jit(solution)/shard_map/ppermute | solution.py:397
  133.0 3.7 %collective-permute-start.13 = (s16[17,32,128]{2,1,0:T(8,128)(2,1)S(1)}, s16[17,32,128]{2,1,0:T(8,128)(2,1)S(1)}, u32[]{:S(2)}, u32[]{:S(2)}) collective-permute-start(s16[17,32,128]{2,1,0:T(8,128)(2,1)S(1)} %get-tuple-element.59), channel_id=1, source_target_pairs={{0,1},{1,0},{2,3},{3,2},{4,5},{5,4},{6,7},{7,6},{8,9},{9,8},{10,11... | collective-permute-start | bytes 417800 | tf_op jit(solution)/shard_map/ppermute | solution.py:391
  137.4 2.4 %collective-permute-done.13.near = s16[17,32,128]{2,1,0:T(8,128)(2,1)S(1)} collective-permute-done((s16[17,32,128]{2,1,0:T(8,128)(2,1)S(1)}, s16[17,32,128]{2,1,0:T(8,128)(2,1)S(1)}, u32[]{:S(2)}, u32[]{:S(2)}) %collective-permute-start.13) | collective-permute-done | bytes 139296 | tf_op jit(solution)/shard_map/ppermute | solution.py:391
  140.3 1.7 %collective-permute-start.15 = (s16[17,32,128]{2,1,0:T(8,128)(2,1)S(1)}, s16[17,32,128]{2,1,0:T(8,128)(2,1)S(1)}, u32[]{:S(2)}, u32[]{:S(2)}) collective-permute-start(s16[17,32,128]{2,1,0:T(8,128)(2,1)S(1)} %get-tuple-element.61.refs_0_), channel_id=1, source_target_pairs={{1,2},{3,0},{2,1},{0,3},{5,6},{7,4},{6,5},{4,7},{9,10},{11,8},{10,... | collective-permute-start | bytes 417800 | tf_op jit(solution)/shard_map/ppermute | solution.py:397
  142.0 3.3 %collective-permute-start.17 = (s16[17,32,128]{2,1,0:T(8,128)(2,1)S(1)}, s16[17,32,128]{2,1,0:T(8,128)(2,1)S(1)}, u32[]{:S(2)}, u32[]{:S(2)}) collective-permute-start(s16[17,32,128]{2,1,0:T(8,128)(2,1)S(1)} %get-tuple-element.62.refs_1_), channel_id=1, source_target_pairs={{0,1},{1,0},{2,3},{3,2},{4,5},{5,4},{6,7},{7,6},{8,9},{9,8},{10,11... | collective-permute-start | bytes 417800 | tf_op jit(solution)/shard_map/ppermute | solution.py:391
  145.3 1.6 %collective-permute-start.20 = (s16[17,32,128]{2,1,0:T(8,128)(2,1)S(1)}, s16[17,32,128]{2,1,0:T(8,128)(2,1)S(1)}, u32[]{:S(2)}, u32[]{:S(2)}) collective-permute-start(s16[17,32,128]{2,1,0:T(8,128)(2,1)S(1)} %get-tuple-element.62.refs_1_), channel_id=1, source_target_pairs={{1,2},{3,0},{2,1},{0,3},{5,6},{7,4},{6,5},{4,7},{9,10},{11,8},{10,... | collective-permute-start | bytes 417800 | tf_op jit(solution)/shard_map/ppermute | solution.py:397
  146.9 3.4 %collective-permute-start.16 = (s16[17,32,128]{2,1,0:T(8,128)(2,1)S(1)}, s16[17,32,128]{2,1,0:T(8,128)(2,1)S(1)}, u32[]{:S(2)}, u32[]{:S(2)}) collective-permute-start(s16[17,32,128]{2,1,0:T(8,128)(2,1)S(1)} %collective-permute-done.15.refs_4_), channel_id=1, source_target_pairs={{0,1},{1,0},{2,3},{3,2},{4,5},{5,4},{6,7},{7,6},{8,9},{9,8},{10,11... | collective-permute-start | bytes 417800 | tf_op jit(solution)/shard_map/ppermute | solution.py:391
  150.4 1.6 %collective-permute-start.18 = (s16[17,32,128]{2,1,0:T(8,128)(2,1)S(1)}, s16[17,32,128]{2,1,0:T(8,128)(2,1)S(1)}, u32[]{:S(2)}, u32[]{:S(2)}) collective-permute-start(s16[17,32,128]{2,1,0:T(8,128)(2,1)S(1)} %collective-permute-done.17.refs_3_), channel_id=1, source_target_pairs={{1,2},{3,0},{2,1},{0,3},{5,6},{7,4},{6,5},{4,7},{9,10},{11,8},{10,... | collective-permute-start | bytes 417800 | tf_op jit(solution)/shard_map/ppermute | solution.py:397
  152.5 1.8 %shard_map.55._ = f32[32,128,128]{2,1,0:T(8,128)} custom-call(s16[17,32,128]{2,1,0:T(8,128)(2,1)S(1)} %get-tuple-element.61.refs_0_, s16[17,32,128]{2,1,0:T(8,128)(2,1)S(1)} %get-tuple-element.62.refs_1_, s16[17,32,128]{2,1,0:T(8,128)(2,1)S(1)} %collective-permute-done.19.refs_2_, s16[17,32,128]{2,1,0:T(8,128)(2,1)S(1)} %collective-permute-done.17.refs_3_, ...), custom_call_target="tpu_custom_call" | custom-call | bytes 835584 | tf_op jit(solution)/shard_map/pallas_call | solution.py:368
  154.3 2.3 %collective-permute-done.18.upper = s16[17,32,128]{2,1,0:T(8,128)(2,1)S(1)} collective-permute-done((s16[17,32,128]{2,1,0:T(8,128)(2,1)S(1)}, s16[17,32,128]{2,1,0:T(8,128)(2,1)S(1)}, u32[]{:S(2)}, u32[]{:S(2)}) %collective-permute-start.18) | collective-permute-done | bytes 139296 | tf_op jit(solution)/shard_map/ppermute | solution.py:397
  (84 shorter events, 17.1 us)
Async XLA Ops:
  0.0 2.2 %copy-start.4 = (s32[2,1024,1]{1,2,0:T(1,128)S(1)}, s32[2,1024,1]{1,2,0:T(1,128)}, u32[]{:S(2)}) copy-start(s32[2,1024,1]{1,2,0:T(1,128)} %param.7) | copy-start | bytes 24580
  0.0 1.9 %copy-start.3 = (f32[2,3,31]{2,0,1:T(2,128)S(1)}, f32[2,3,31]{2,0,1:T(2,128)}, u32[]{:S(2)}) copy-start(f32[2,3,31]{2,0,1:T(2,128)} %param.6) | copy-start | bytes 2236
  2.5 14.7 %collective-permute-start.3 = (f32[2,128]{1,0:T(2,128)S(1)}, f32[2,128]{1,0:T(2,128)S(1)}, u32[]{:S(2)}, u32[]{:S(2)}) collective-permute-start(f32[2,128]{1,0:T(2,128)S(1)} %select_maximum_fusion), channel_id=1, source_target_pairs={{1,2},{3,0},{2,1},{0,3},{5,6},{7,4},{6,5},{4,7},{9,10},{11,8},{10,... | collective-permute-start | bytes 3080 | tf_op jit(solution)/shard_map/ppermute | solution.py:397
  5.5 11.7 %collective-permute-start.2 = (f32[2,128]{1,0:T(2,128)S(1)}, f32[2,128]{1,0:T(2,128)S(1)}, u32[]{:S(2)}, u32[]{:S(2)}) collective-permute-start(f32[2,128]{1,0:T(2,128)S(1)} %select_maximum_fusion), channel_id=1, source_target_pairs={{0,1},{1,0},{2,3},{3,2},{4,5},{5,4},{6,7},{7,6},{8,9},{9,8},{10,11... | collective-permute-start | bytes 3080 | tf_op jit(solution)/shard_map/ppermute | solution.py:391
  5.7 11.6 %collective-permute-start.4 = (f32[2,128]{1,0:T(2,128)S(1)}, f32[2,128]{1,0:T(2,128)S(1)}, u32[]{:S(2)}, u32[]{:S(2)}) collective-permute-start(f32[2,128]{1,0:T(2,128)S(1)} %select_maximum_fusion), channel_id=1, source_target_pairs={{0,2},{1,3},{2,0},{3,1},{4,6},{5,7},{6,4},{7,5},{8,10},{9,11},{10,... | collective-permute-start | bytes 3080 | tf_op jit(solution)/shard_map/ppermute | solution.py:435
  7.2 10.1 %collective-permute-start = (bf16[64,16,128]{2,1,0:T(8,128)(2,1)S(1)}, bf16[64,16,128]{2,1,0:T(8,128)(2,1)S(1)}, u32[]{:S(2)}, u32[]{:S(2)}) collective-permute-start(bf16[64,16,128]{2,1,0:T(8,128)(2,1)S(1)} %get-tuple-element.36), channel_id=1, source_target_pairs={{0,4},{4,0},{8,12},{12,8},{16,20},{20,16},{24,28},{28,24},{32,36},... | collective-permute-start | bytes 786440 | tf_op jit(solution)/shard_map/ppermute | solution.py:391
  7.2 10.1 %collective-permute-start.1 = (bf16[64,16,128]{2,1,0:T(8,128)(2,1)S(1)}, bf16[64,16,128]{2,1,0:T(8,128)(2,1)S(1)}, u32[]{:S(2)}, u32[]{:S(2)}) collective-permute-start(bf16[64,16,128]{2,1,0:T(8,128)(2,1)S(1)} %get-tuple-element.37), channel_id=1, source_target_pairs={{4,8},{12,16},{20,24},{28,32},{36,40},{44,48},{52,56},{60,64},{68,... | collective-permute-start | bytes 786440 | tf_op jit(solution)/shard_map/ppermute | solution.py:397
  17.4 62.5 %all-to-all-start = ((bf16[128,4,32,128]{3,2,1,0:T(8,128)(2,1)}), bf16[128,4,32,128]{3,2,1,0:T(8,128)(2,1)}, u32[]{:S(2)}, u32[]{:S(2)}) async-start(bf16[128,4,32,128]{3,2,1,0:T(8,128)(2,1)} %bitcast.43), calls=%async_computation | async-start | bytes 8388608 | tf_op jit(solution)/shard_map/all_to_all | solution.py:456
  89.3 3.4 %collective-permute-start.5 = (s16[65,32,128]{2,1,0:T(8,128)(2,1)S(1)}, s16[65,32,128]{2,1,0:T(8,128)(2,1)S(1)}, u32[]{:S(2)}, u32[]{:S(2)}) collective-permute-start(s16[65,32,128]{2,1,0:T(8,128)(2,1)S(1)} %get-tuple-element.46), channel_id=1, source_target_pairs={{0,4},{4,0},{8,12},{12,8},{16,20},{20,16},{24,28},{28,24},{32,36},... | collective-permute-start | bytes 1597448 | tf_op jit(solution)/shard_map/ppermute | solution.py:391
  89.8 12.7 %collective-permute-start.6 = (s16[65,32,128]{2,1,0:T(8,128)(2,1)S(1)}, s16[65,32,128]{2,1,0:T(8,128)(2,1)S(1)}, u32[]{:S(2)}, u32[]{:S(2)}) collective-permute-start(s16[65,32,128]{2,1,0:T(8,128)(2,1)S(1)} %get-tuple-element.48), channel_id=1, source_target_pairs={{4,8},{12,16},{20,24},{28,32},{36,40},{44,48},{52,56},{60,64},{68,... | collective-permute-start | bytes 1597448 | tf_op jit(solution)/shard_map/ppermute | solution.py:397
  93.5 11.2 %collective-permute-start.7 = (s16[33,32,128]{2,1,0:T(8,128)(2,1)S(1)}, s16[33,32,128]{2,1,0:T(8,128)(2,1)S(1)}, u32[]{:S(2)}, u32[]{:S(2)}) collective-permute-start(s16[33,32,128]{2,1,0:T(8,128)(2,1)S(1)} %get-tuple-element.50), channel_id=1, source_target_pairs={{0,1},{1,0},{2,3},{3,2},{4,5},{5,4},{6,7},{7,6},{8,9},{9,8},{10,11... | collective-permute-start | bytes 811016 | tf_op jit(solution)/shard_map/ppermute | solution.py:391
  94.2 10.5 %collective-permute-start.8 = (s16[33,32,128]{2,1,0:T(8,128)(2,1)S(1)}, s16[33,32,128]{2,1,0:T(8,128)(2,1)S(1)}, u32[]{:S(2)}, u32[]{:S(2)}) collective-permute-start(s16[33,32,128]{2,1,0:T(8,128)(2,1)S(1)} %get-tuple-element.51), channel_id=1, source_target_pairs={{1,2},{2,1},{5,6},{6,5},{9,10},{10,9},{13,14},{14,13},{17,18},{18,... | collective-permute-start | bytes 811016 | tf_op jit(solution)/shard_map/ppermute | solution.py:397
  103.4 6.8 %collective-permute-start.9 = (s16[33,32,128]{2,1,0:T(8,128)(2,1)S(1)}, s16[33,32,128]{2,1,0:T(8,128)(2,1)S(1)}, u32[]{:S(2)}, u32[]{:S(2)}) collective-permute-start(s16[33,32,128]{2,1,0:T(8,128)(2,1)S(1)} %get-tuple-element.52), channel_id=1, source_target_pairs={{0,1},{1,0},{2,3},{3,2},{4,5},{5,4},{6,7},{7,6},{8,9},{9,8},{10,11... | collective-permute-start | bytes 811016 | tf_op jit(solution)/shard_map/ppermute | solution.py:391
  104.0 6.2 %collective-permute-start.10 = (s16[33,32,128]{2,1,0:T(8,128)(2,1)S(1)}, s16[33,32,128]{2,1,0:T(8,128)(2,1)S(1)}, u32[]{:S(2)}, u32[]{:S(2)}) collective-permute-start(s16[33,32,128]{2,1,0:T(8,128)(2,1)S(1)} %get-tuple-element.53), channel_id=1, source_target_pairs={{1,2},{2,1},{5,6},{6,5},{9,10},{10,9},{13,14},{14,13},{17,18},{18,... | collective-permute-start | bytes 811016 | tf_op jit(solution)/shard_map/ppermute | solution.py:397
  122.2 3.1 %collective-permute-start.11 = (s16[65,16,128]{2,1,0:T(8,128)(2,1)S(1)}, s16[65,16,128]{2,1,0:T(8,128)(2,1)S(1)}, u32[]{:S(2)}, u32[]{:S(2)}) collective-permute-start(s16[65,16,128]{2,1,0:T(8,128)(2,1)S(1)} %get-tuple-element.56), channel_id=1, source_target_pairs={{0,4},{4,0},{8,12},{12,8},{16,20},{20,16},{24,28},{28,24},{32,36},... | collective-permute-start | bytes 798728 | tf_op jit(solution)/shard_map/ppermute | solution.py:391
  122.3 9.8 %collective-permute-start.12 = (s16[65,16,128]{2,1,0:T(8,128)(2,1)S(1)}, s16[65,16,128]{2,1,0:T(8,128)(2,1)S(1)}, u32[]{:S(2)}, u32[]{:S(2)}) collective-permute-start(s16[65,16,128]{2,1,0:T(8,128)(2,1)S(1)} %get-tuple-element.57), channel_id=1, source_target_pairs={{4,8},{12,16},{20,24},{28,32},{36,40},{44,48},{52,56},{60,64},{68,... | collective-permute-start | bytes 798728 | tf_op jit(solution)/shard_map/ppermute | solution.py:397
  133.0 6.8 %collective-permute-start.13 = (s16[17,32,128]{2,1,0:T(8,128)(2,1)S(1)}, s16[17,32,128]{2,1,0:T(8,128)(2,1)S(1)}, u32[]{:S(2)}, u32[]{:S(2)}) collective-permute-start(s16[17,32,128]{2,1,0:T(8,128)(2,1)S(1)} %get-tuple-element.59), channel_id=1, source_target_pairs={{0,1},{1,0},{2,3},{3,2},{4,5},{5,4},{6,7},{7,6},{8,9},{9,8},{10,11... | collective-permute-start | bytes 417800 | tf_op jit(solution)/shard_map/ppermute | solution.py:391
  136.8 3.0 %collective-permute-start.14 = (s16[17,32,128]{2,1,0:T(8,128)(2,1)S(1)}, s16[17,32,128]{2,1,0:T(8,128)(2,1)S(1)}, u32[]{:S(2)}, u32[]{:S(2)}) collective-permute-start(s16[17,32,128]{2,1,0:T(8,128)(2,1)S(1)} %get-tuple-element.60), channel_id=1, source_target_pairs={{1,2},{2,1},{5,6},{6,5},{9,10},{10,9},{13,14},{14,13},{17,18},{18,... | collective-permute-start | bytes 417800 | tf_op jit(solution)/shard_map/ppermute | solution.py:397
  140.3 6.7 %collective-permute-start.15 = (s16[17,32,128]{2,1,0:T(8,128)(2,1)S(1)}, s16[17,32,128]{2,1,0:T(8,128)(2,1)S(1)}, u32[]{:S(2)}, u32[]{:S(2)}) collective-permute-start(s16[17,32,128]{2,1,0:T(8,128)(2,1)S(1)} %get-tuple-element.61.refs_0_), channel_id=1, source_target_pairs={{1,2},{3,0},{2,1},{0,3},{5,6},{7,4},{6,5},{4,7},{9,10},{11,8},{10,... | collective-permute-start | bytes 417800 | tf_op jit(solution)/shard_map/ppermute | solution.py:397
  142.0 8.4 %collective-permute-start.17 = (s16[17,32,128]{2,1,0:T(8,128)(2,1)S(1)}, s16[17,32,128]{2,1,0:T(8,128)(2,1)S(1)}, u32[]{:S(2)}, u32[]{:S(2)}) collective-permute-start(s16[17,32,128]{2,1,0:T(8,128)(2,1)S(1)} %get-tuple-element.62.refs_1_), channel_id=1, source_target_pairs={{0,1},{1,0},{2,3},{3,2},{4,5},{5,4},{6,7},{7,6},{8,9},{9,8},{10,11... | collective-permute-start | bytes 417800 | tf_op jit(solution)/shard_map/ppermute | solution.py:391
  145.3 6.7 %collective-permute-start.19 = (s16[17,32,128]{2,1,0:T(8,128)(2,1)S(1)}, s16[17,32,128]{2,1,0:T(8,128)(2,1)S(1)}, u32[]{:S(2)}, u32[]{:S(2)}) collective-permute-start(s16[17,32,128]{2,1,0:T(8,128)(2,1)S(1)} %get-tuple-element.61.refs_0_), channel_id=1, source_target_pairs={{0,1},{1,0},{2,3},{3,2},{4,5},{5,4},{6,7},{7,6},{8,9},{9,8},{10,11... | collective-permute-start | bytes 417800 | tf_op jit(solution)/shard_map/ppermute | solution.py:391
  145.3 7.2 %collective-permute-start.20 = (s16[17,32,128]{2,1,0:T(8,128)(2,1)S(1)}, s16[17,32,128]{2,1,0:T(8,128)(2,1)S(1)}, u32[]{:S(2)}, u32[]{:S(2)}) collective-permute-start(s16[17,32,128]{2,1,0:T(8,128)(2,1)S(1)} %get-tuple-element.62.refs_1_), channel_id=1, source_target_pairs={{1,2},{3,0},{2,1},{0,3},{5,6},{7,4},{6,5},{4,7},{9,10},{11,8},{10,... | collective-permute-start | bytes 417800 | tf_op jit(solution)/shard_map/ppermute | solution.py:397
  146.9 7.4 %collective-permute-start.16 = (s16[17,32,128]{2,1,0:T(8,128)(2,1)S(1)}, s16[17,32,128]{2,1,0:T(8,128)(2,1)S(1)}, u32[]{:S(2)}, u32[]{:S(2)}) collective-permute-start(s16[17,32,128]{2,1,0:T(8,128)(2,1)S(1)} %collective-permute-done.15.refs_4_), channel_id=1, source_target_pairs={{0,1},{1,0},{2,3},{3,2},{4,5},{5,4},{6,7},{7,6},{8,9},{9,8},{10,11... | collective-permute-start | bytes 417800 | tf_op jit(solution)/shard_map/ppermute | solution.py:391
  150.4 6.3 %collective-permute-start.18 = (s16[17,32,128]{2,1,0:T(8,128)(2,1)S(1)}, s16[17,32,128]{2,1,0:T(8,128)(2,1)S(1)}, u32[]{:S(2)}, u32[]{:S(2)}) collective-permute-start(s16[17,32,128]{2,1,0:T(8,128)(2,1)S(1)} %collective-permute-done.17.refs_3_), channel_id=1, source_target_pairs={{1,2},{3,0},{2,1},{0,3},{5,6},{7,4},{6,5},{4,7},{9,10},{11,8},{10,... | collective-permute-start | bytes 417800 | tf_op jit(solution)/shard_map/ppermute | solution.py:397
  (3 other events, 4.5 us)

commit v4 on v2

--- a/solution.py
+++ b/solution.py
@@ -432,8 +432,8 @@
         [normed.reshape(views_dev, 3 * TAPS), where.astype(F32)], axis=1
     )
     packed = jnp.pad(packed, ((0, 0), (0, 128 - packed.shape[1])))
-    across = lax.ppermute(packed, "view", [(i, (i + 2) % groups) for i in range(groups)])
-    around = [packed, swap_near(packed, "view"), swap_far(packed, "view", True), across]
+    mine = jnp.concatenate([packed, swap_near(packed, "view")])
+    around = jnp.split(jnp.concatenate([mine, swap_far(mine, "view", True)]), groups)
     order = jnp.stack([group, group ^ 1, (group + 2 * (group % 2) - 1) % groups, (group + 2) % groups])
     here = order[:, None] == jnp.arange(groups)[None, :]
     packed = jnp.sum(jnp.where(here[:, :, None, None], jnp.stack(around)[:, None], 0.0), axis=0)

time: 158 us -> 155 us (0.981)
  starting transfers between devices: 46.4 us -> 43.1 us
    all_to_all x1, starting transfers between devices: 10.6 us -> 8.11 us  [per_device(): got = lax.all_to_all(sending, BOTH, 0, 0, tiled=True)]
  transfers between devices with their start and end apart: 22 -> 21, of which waited for: 7 -> 7; matrix products, arithmetic and copies ran while one was open for 3% -> 3% of each run, Pallas kernels for 7% -> 8%
where the time goes in v4:
time: 155 us; the launch traced here: 154 us
  waiting for transfers between devices  66.5 us (43%)
  starting transfers between devices  43.1 us (28%)
  Pallas kernels  34.2 us (22%)
  local copies, waits for them, and re-layouts  6.14 us (4%)
  other arithmetic  2.52 us (2%)
    all_to_all x1, waiting for transfers between devices, per_device(): got = lax.all_to_all(sending, BOTH, 0, 0, tiled=True)  41.4 us
    pallas_call x10, Pallas kernels, call(): pl.pallas_call(kernel, out_shape=out_shape, in_specs=[SMEM] * scalars + [...  33.3 us
    ppermute x10, starting transfers between devices, swap_far(): return lax.ppermute(a, axis, pairs + [(j, i) for i, j in pairs])  21.1 us
    ppermute x10, waiting for transfers between devices, swap_far(): return lax.ppermute(a, axis, pairs + [(j, i) for i, j in pairs])  17.3 us
    ppermute x10, starting transfers between devices, swap_near(): lax.ppermute(a, axis, [(i, i ^ 1) for i in range(lax.axis_size(axis))])  13.9 us
    all_to_all x1, starting transfers between devices, per_device(): got = lax.all_to_all(sending, BOTH, 0, 0, tiled=True)  8.11 us
    ppermute x10, waiting for transfers between devices, swap_near(): lax.ppermute(a, axis, [(i, i ^ 1) for i in range(lax.axis_size(axis))])  7.89 us
    unnamed x10, local copies, waits for them, and re-layouts  4.51 us
  transfers between devices with their start and end apart: 21, of which 7 were waited for; matrix products, arithmetic and copies ran while one was open for 3% of the time, Pallas kernels for 8%

profile of v4, /device:TPU:2, one launch (start us, length us, event | category | flops | bytes accessed | tf_op | source)
XLA Modules:
  0.0 154.5 jit_solution(2675232804903338036)
XLA Ops:
  0.0 1.6 %copy-done = f32[32,128,128]{2,1,0:T(8,128)S(1)} copy-done((f32[32,128,128]{2,1,0:T(8,128)S(1)}, f32[32,128,128]{2,1,0:T(8,128)}, u32[]{:S(2)}) %copy-start) | copy-done | bytes 2097176
  2.5 1.6 %collective-permute-start.2 = (f32[2,128]{1,0:T(2,128)S(1)}, f32[2,128]{1,0:T(2,128)S(1)}, u32[]{:S(2)}, u32[]{:S(2)}) collective-permute-start(f32[2,128]{1,0:T(2,128)S(1)} %select_maximum_fusion), channel_id=1, source_target_pairs={{0,1},{1,0},{2,3},{3,2},{4,5},{5,4},{6,7},{7,6},{8,9},{9,8},{10,11... | collective-permute-start | bytes 3080 | tf_op jit(solution)/shard_map/ppermute | solution.py:391
  4.1 6.0 %collective-permute-start.1 = (bf16[64,16,128]{2,1,0:T(8,128)(2,1)S(1)}, bf16[64,16,128]{2,1,0:T(8,128)(2,1)S(1)}, u32[]{:S(2)}, u32[]{:S(2)}) collective-permute-start(bf16[64,16,128]{2,1,0:T(8,128)(2,1)S(1)} %get-tuple-element.37), channel_id=1, source_target_pairs={{4,8},{12,16},{20,24},{28,32},{36,40},{44,48},{52,56},{60,64},{68,... | collective-permute-start | bytes 786440 | tf_op jit(solution)/shard_map/ppermute | solution.py:397
  10.3 2.3 %collective-permute-start.3 = (f32[4,128]{1,0:T(4,128)S(1)}, f32[4,128]{1,0:T(4,128)S(1)}, u32[]{:S(2)}, u32[]{:S(2)}) collective-permute-start(f32[4,128]{1,0:T(4,128)S(1)} %pad_maximum_fusion.7), channel_id=1, source_target_pairs={{1,2},{3,0},{2,1},{0,3},{5,6},{7,4},{6,5},{4,7},{9,10},{11,8},{10,... | collective-permute-start | bytes 6152 | tf_op jit(solution)/shard_map/ppermute | solution.py:397
  12.7 3.8 %shard_map.46 = bf16[32,4,2,2,32,128]{5,4,3,2,1,0:T(8,128)(2,1)} custom-call(bf16[2,32,2,128,128]{4,3,2,1,0:T(8,128)(2,1)} %bitcast.47), custom_call_target="tpu_custom_call" | custom-call | bytes 4194304 | tf_op jit(solution)/shard_map/pallas_call | solution.py:368
  16.6 8.1 %all-to-all-start = ((bf16[128,4,32,128]{3,2,1,0:T(8,128)(2,1)}), bf16[128,4,32,128]{3,2,1,0:T(8,128)(2,1)}, u32[]{:S(2)}, u32[]{:S(2)}) async-start(bf16[128,4,32,128]{3,2,1,0:T(8,128)(2,1)} %bitcast.46), calls=%async_computation | async-start | bytes 8388608 | tf_op jit(solution)/shard_map/all_to_all | solution.py:456
  29.4 4.5 %shard_map.48.blurred = bf16[8,1024,128]{2,1,0:T(8,128)(2,1)S(1)} custom-call(bf16[64,16,128]{2,1,0:T(8,128)(2,1)S(1)} %collective-permute-done.near, f32[64,32,128]{2,1,0:T(8,128)S(1)} %get-tuple-element.42.middle, bf16[64,16,128]{2,1,0:T(8,128)(2,1)S(1)} %collective-permute-done.1.far, bf16[256,128]{1,0:T(8,128)(2,1)S(1)} %pad_maximum_fusion.3.ax, ...), custom_call_target="tpu_custom_call" | custom-call | flops 4000000000 | bytes 2228224 | tf_op jit(solution)/shard_map/pallas_call | solution.py:368
  35.3 41.4 %all-to-all-done = bf16[128,4,32,128]{3,2,1,0:T(8,128)(2,1)} async-done(((bf16[128,4,32,128]{3,2,1,0:T(8,128)(2,1)}), bf16[128,4,32,128]{3,2,1,0:T(8,128)(2,1)}, u32[]{:S(2)}, u32[]{:S(2)}) %all-to-all-start) | async-done | bytes 4194336 | tf_op jit(solution)/shard_map/all_to_all | solution.py:456
  78.2 7.9 %shard_map.49 = (f32[64,64,128]{2,1,0:T(8,128)S(1)}, s16[65,32,128]{2,1,0:T(8,128)(2,1)S(1)}, s16[65,32,128]{2,1,0:T(8,128)(2,1)S(1)}) custom-call(s32[256]{0:T(256)S(1)} %reshape.94.where, bf16[8,1024,128]{2,1,0:T(8,128)(2,1)S(1)} %copy-done.2, bf16[512,32,128]{2,1,0:T(8,128)(2,1)} %bitcast.21.got, bf16[128,256]{1,0:T(8,128)(2,1)S(1)} %pad_maximum_fusion.5.axt, ...), custom_call_target="tpu_custom_call" | custom-call | flops 4000000000 | bytes 6947840 | tf_op jit(solution)/shard_map/pallas_call | solution.py:368
  86.6 2.9 %collective-permute-start.5 = (s16[65,32,128]{2,1,0:T(8,128)(2,1)S(1)}, s16[65,32,128]{2,1,0:T(8,128)(2,1)S(1)}, u32[]{:S(2)}, u32[]{:S(2)}) collective-permute-start(s16[65,32,128]{2,1,0:T(8,128)(2,1)S(1)} %get-tuple-element.48), channel_id=1, source_target_pairs={{4,8},{12,16},{20,24},{28,32},{36,40},{44,48},{52,56},{60,64},{68,... | collective-permute-start | bytes 1597448 | tf_op jit(solution)/shard_map/ppermute | solution.py:397
  91.7 7.5 %collective-permute-done.5.got = s16[65,32,128]{2,1,0:T(8,128)(2,1)S(1)} collective-permute-done((s16[65,32,128]{2,1,0:T(8,128)(2,1)S(1)}, s16[65,32,128]{2,1,0:T(8,128)(2,1)S(1)}, u32[]{:S(2)}, u32[]{:S(2)}) %collective-permute-start.5) | collective-permute-done | bytes 532512 | tf_op jit(solution)/shard_map/ppermute | solution.py:397
  101.4 5.5 %collective-permute-done.8.got_fn = s16[33,32,128]{2,1,0:T(8,128)(2,1)S(1)} collective-permute-done((s16[33,32,128]{2,1,0:T(8,128)(2,1)S(1)}, s16[33,32,128]{2,1,0:T(8,128)(2,1)S(1)}, u32[]{:S(2)}, u32[]{:S(2)}) %collective-permute-start.8) | collective-permute-done | bytes 270368 | tf_op jit(solution)/shard_map/ppermute | solution.py:391
  106.9 12.3 %shard_map.52 = (f32[64,32,128]{2,1,0:T(8,128)S(1)}, f32[64,64,128]{2,1,0:T(8,128)S(1)}, s16[65,16,128]{2,1,0:T(8,128)(2,1)S(1)}, s16[65,16,128]{2,1,0:T(8,128)(2,1)S(1)}) custom-call(s32[256]{0:T(256)S(1)} %reshape.94.where, bf16[64,16,128]{2,1,0:T(8,128)(2,1)S(1)} %collective-permute-done.near, f32[64,32,128]{2,1,0:T(8,128)S(1)} %get-tuple-element.42.middle, ...), custom_call_target="tpu_custom_call" | custom-call | flops 8000000000 | bytes 10257408 | tf_op jit(solution)/shard_map/pallas_call | solution.py:368
  119.3 3.0 %collective-permute-start.11 = (s16[65,16,128]{2,1,0:T(8,128)(2,1)S(1)}, s16[65,16,128]{2,1,0:T(8,128)(2,1)S(1)}, u32[]{:S(2)}, u32[]{:S(2)}) collective-permute-start(s16[65,16,128]{2,1,0:T(8,128)(2,1)S(1)} %get-tuple-element.57), channel_id=1, source_target_pairs={{4,8},{12,16},{20,24},{28,32},{36,40},{44,48},{52,56},{60,64},{68,... | collective-permute-start | bytes 798728 | tf_op jit(solution)/shard_map/ppermute | solution.py:397
  122.3 6.8 %collective-permute-done.11.far = s16[65,16,128]{2,1,0:T(8,128)(2,1)S(1)} collective-permute-done((s16[65,16,128]{2,1,0:T(8,128)(2,1)S(1)}, s16[65,16,128]{2,1,0:T(8,128)(2,1)S(1)}, u32[]{:S(2)}, u32[]{:S(2)}) %collective-permute-start.11) | collective-permute-done | bytes 266272 | tf_op jit(solution)/shard_map/ppermute | solution.py:397
  129.8 3.7 %collective-permute-start.12 = (s16[17,32,128]{2,1,0:T(8,128)(2,1)S(1)}, s16[17,32,128]{2,1,0:T(8,128)(2,1)S(1)}, u32[]{:S(2)}, u32[]{:S(2)}) collective-permute-start(s16[17,32,128]{2,1,0:T(8,128)(2,1)S(1)} %get-tuple-element.59), channel_id=1, source_target_pairs={{0,1},{1,0},{2,3},{3,2},{4,5},{5,4},{6,7},{7,6},{8,9},{9,8},{10,11... | collective-permute-start | bytes 417800 | tf_op jit(solution)/shard_map/ppermute | solution.py:391
  134.2 2.4 %collective-permute-done.12.near = s16[17,32,128]{2,1,0:T(8,128)(2,1)S(1)} collective-permute-done((s16[17,32,128]{2,1,0:T(8,128)(2,1)S(1)}, s16[17,32,128]{2,1,0:T(8,128)(2,1)S(1)}, u32[]{:S(2)}, u32[]{:S(2)}) %collective-permute-start.12) | collective-permute-done | bytes 139296 | tf_op jit(solution)/shard_map/ppermute | solution.py:391
  137.1 1.7 %collective-permute-start.14 = (s16[17,32,128]{2,1,0:T(8,128)(2,1)S(1)}, s16[17,32,128]{2,1,0:T(8,128)(2,1)S(1)}, u32[]{:S(2)}, u32[]{:S(2)}) collective-permute-start(s16[17,32,128]{2,1,0:T(8,128)(2,1)S(1)} %get-tuple-element.61.refs_0_), channel_id=1, source_target_pairs={{1,2},{3,0},{2,1},{0,3},{5,6},{7,4},{6,5},{4,7},{9,10},{11,8},{10,... | collective-permute-start | bytes 417800 | tf_op jit(solution)/shard_map/ppermute | solution.py:397
  138.8 3.3 %collective-permute-start.16 = (s16[17,32,128]{2,1,0:T(8,128)(2,1)S(1)}, s16[17,32,128]{2,1,0:T(8,128)(2,1)S(1)}, u32[]{:S(2)}, u32[]{:S(2)}) collective-permute-start(s16[17,32,128]{2,1,0:T(8,128)(2,1)S(1)} %get-tuple-element.62.refs_1_), channel_id=1, source_target_pairs={{0,1},{1,0},{2,3},{3,2},{4,5},{5,4},{6,7},{7,6},{8,9},{9,8},{10,11... | collective-permute-start | bytes 417800 | tf_op jit(solution)/shard_map/ppermute | solution.py:391
  142.1 1.6 %collective-permute-start.19 = (s16[17,32,128]{2,1,0:T(8,128)(2,1)S(1)}, s16[17,32,128]{2,1,0:T(8,128)(2,1)S(1)}, u32[]{:S(2)}, u32[]{:S(2)}) collective-permute-start(s16[17,32,128]{2,1,0:T(8,128)(2,1)S(1)} %get-tuple-element.62.refs_1_), channel_id=1, source_target_pairs={{1,2},{3,0},{2,1},{0,3},{5,6},{7,4},{6,5},{4,7},{9,10},{11,8},{10,... | collective-permute-start | bytes 417800 | tf_op jit(solution)/shard_map/ppermute | solution.py:397
  143.7 3.4 %collective-permute-start.15 = (s16[17,32,128]{2,1,0:T(8,128)(2,1)S(1)}, s16[17,32,128]{2,1,0:T(8,128)(2,1)S(1)}, u32[]{:S(2)}, u32[]{:S(2)}) collective-permute-start(s16[17,32,128]{2,1,0:T(8,128)(2,1)S(1)} %collective-permute-done.14.refs_4_), channel_id=1, source_target_pairs={{0,1},{1,0},{2,3},{3,2},{4,5},{5,4},{6,7},{7,6},{8,9},{9,8},{10,11... | collective-permute-start | bytes 417800 | tf_op jit(solution)/shard_map/ppermute | solution.py:391
  147.2 1.6 %collective-permute-start.17 = (s16[17,32,128]{2,1,0:T(8,128)(2,1)S(1)}, s16[17,32,128]{2,1,0:T(8,128)(2,1)S(1)}, u32[]{:S(2)}, u32[]{:S(2)}) collective-permute-start(s16[17,32,128]{2,1,0:T(8,128)(2,1)S(1)} %collective-permute-done.16.refs_3_), channel_id=1, source_target_pairs={{1,2},{3,0},{2,1},{0,3},{5,6},{7,4},{6,5},{4,7},{9,10},{11,8},{10,... | collective-permute-start | bytes 417800 | tf_op jit(solution)/shard_map/ppermute | solution.py:397
  149.3 1.8 %shard_map.55._ = f32[32,128,128]{2,1,0:T(8,128)} custom-call(s16[17,32,128]{2,1,0:T(8,128)(2,1)S(1)} %get-tuple-element.61.refs_0_, s16[17,32,128]{2,1,0:T(8,128)(2,1)S(1)} %get-tuple-element.62.refs_1_, s16[17,32,128]{2,1,0:T(8,128)(2,1)S(1)} %collective-permute-done.18.refs_2_, s16[17,32,128]{2,1,0:T(8,128)(2,1)S(1)} %collective-permute-done.16.refs_3_, ...), custom_call_target="tpu_custom_call" | custom-call | bytes 835584 | tf_op jit(solution)/shard_map/pallas_call | solution.py:368
  151.1 2.3 %collective-permute-done.17.upper = s16[17,32,128]{2,1,0:T(8,128)(2,1)S(1)} collective-permute-done((s16[17,32,128]{2,1,0:T(8,128)(2,1)S(1)}, s16[17,32,128]{2,1,0:T(8,128)(2,1)S(1)}, u32[]{:S(2)}, u32[]{:S(2)}) %collective-permute-start.17) | collective-permute-done | bytes 139296 | tf_op jit(solution)/shard_map/ppermute | solution.py:397
  (85 shorter events, 16.7 us)
Async XLA Ops:
  0.0 2.2 %copy-start.4 = (s32[2,1024,1]{1,2,0:T(1,128)S(1)}, s32[2,1024,1]{1,2,0:T(1,128)}, u32[]{:S(2)}) copy-start(s32[2,1024,1]{1,2,0:T(1,128)} %param.7) | copy-start | bytes 24580
  0.0 1.9 %copy-start.3 = (f32[2,3,31]{2,0,1:T(2,128)S(1)}, f32[2,3,31]{2,0,1:T(2,128)}, u32[]{:S(2)}) copy-start(f32[2,3,31]{2,0,1:T(2,128)} %param.6) | copy-start | bytes 2236
  0.0 1.6 %copy-start = (f32[32,128,128]{2,1,0:T(8,128)S(1)}, f32[32,128,128]{2,1,0:T(8,128)}, u32[]{:S(2)}) copy-start(f32[32,128,128]{2,1,0:T(8,128)} %estimate.1) | copy-start | bytes 6291460
  2.5 7.8 %collective-permute-start.2 = (f32[2,128]{1,0:T(2,128)S(1)}, f32[2,128]{1,0:T(2,128)S(1)}, u32[]{:S(2)}, u32[]{:S(2)}) collective-permute-start(f32[2,128]{1,0:T(2,128)S(1)} %select_maximum_fusion), channel_id=1, source_target_pairs={{0,1},{1,0},{2,3},{3,2},{4,5},{5,4},{6,7},{7,6},{8,9},{9,8},{10,11... | collective-permute-start | bytes 3080 | tf_op jit(solution)/shard_map/ppermute | solution.py:391
  4.1 12.5 %collective-permute-start = (bf16[64,16,128]{2,1,0:T(8,128)(2,1)S(1)}, bf16[64,16,128]{2,1,0:T(8,128)(2,1)S(1)}, u32[]{:S(2)}, u32[]{:S(2)}) collective-permute-start(bf16[64,16,128]{2,1,0:T(8,128)(2,1)S(1)} %get-tuple-element.36), channel_id=1, source_target_pairs={{0,4},{4,0},{8,12},{12,8},{16,20},{20,16},{24,28},{28,24},{32,36},... | collective-permute-start | bytes 786440 | tf_op jit(solution)/shard_map/ppermute | solution.py:391
  4.1 12.5 %collective-permute-start.1 = (bf16[64,16,128]{2,1,0:T(8,128)(2,1)S(1)}, bf16[64,16,128]{2,1,0:T(8,128)(2,1)S(1)}, u32[]{:S(2)}, u32[]{:S(2)}) collective-permute-start(bf16[64,16,128]{2,1,0:T(8,128)(2,1)S(1)} %get-tuple-element.37), channel_id=1, source_target_pairs={{4,8},{12,16},{20,24},{28,32},{36,40},{44,48},{52,56},{60,64},{68,... | collective-permute-start | bytes 786440 | tf_op jit(solution)/shard_map/ppermute | solution.py:397
  10.3 6.1 %collective-permute-start.3 = (f32[4,128]{1,0:T(4,128)S(1)}, f32[4,128]{1,0:T(4,128)S(1)}, u32[]{:S(2)}, u32[]{:S(2)}) collective-permute-start(f32[4,128]{1,0:T(4,128)S(1)} %pad_maximum_fusion.7), channel_id=1, source_target_pairs={{1,2},{3,0},{2,1},{0,3},{5,6},{7,4},{6,5},{4,7},{9,10},{11,8},{10,... | collective-permute-start | bytes 6152 | tf_op jit(solution)/shard_map/ppermute | solution.py:397
  16.6 60.1 %all-to-all-start = ((bf16[128,4,32,128]{3,2,1,0:T(8,128)(2,1)}), bf16[128,4,32,128]{3,2,1,0:T(8,128)(2,1)}, u32[]{:S(2)}, u32[]{:S(2)}) async-start(bf16[128,4,32,128]{3,2,1,0:T(8,128)(2,1)} %bitcast.46), calls=%async_computation | async-start | bytes 8388608 | tf_op jit(solution)/shard_map/all_to_all | solution.py:456
  86.1 3.4 %collective-permute-start.4 = (s16[65,32,128]{2,1,0:T(8,128)(2,1)S(1)}, s16[65,32,128]{2,1,0:T(8,128)(2,1)S(1)}, u32[]{:S(2)}, u32[]{:S(2)}) collective-permute-start(s16[65,32,128]{2,1,0:T(8,128)(2,1)S(1)} %get-tuple-element.46), channel_id=1, source_target_pairs={{0,4},{4,0},{8,12},{12,8},{16,20},{20,16},{24,28},{28,24},{32,36},... | collective-permute-start | bytes 1597448 | tf_op jit(solution)/shard_map/ppermute | solution.py:391
  86.6 12.7 %collective-permute-start.5 = (s16[65,32,128]{2,1,0:T(8,128)(2,1)S(1)}, s16[65,32,128]{2,1,0:T(8,128)(2,1)S(1)}, u32[]{:S(2)}, u32[]{:S(2)}) collective-permute-start(s16[65,32,128]{2,1,0:T(8,128)(2,1)S(1)} %get-tuple-element.48), channel_id=1, source_target_pairs={{4,8},{12,16},{20,24},{28,32},{36,40},{44,48},{52,56},{60,64},{68,... | collective-permute-start | bytes 1597448 | tf_op jit(solution)/shard_map/ppermute | solution.py:397
  90.3 11.0 %collective-permute-start.6 = (s16[33,32,128]{2,1,0:T(8,128)(2,1)S(1)}, s16[33,32,128]{2,1,0:T(8,128)(2,1)S(1)}, u32[]{:S(2)}, u32[]{:S(2)}) collective-permute-start(s16[33,32,128]{2,1,0:T(8,128)(2,1)S(1)} %get-tuple-element.50), channel_id=1, source_target_pairs={{0,1},{1,0},{2,3},{3,2},{4,5},{5,4},{6,7},{7,6},{8,9},{9,8},{10,11... | collective-permute-start | bytes 811016 | tf_op jit(solution)/shard_map/ppermute | solution.py:391
  91.0 10.3 %collective-permute-start.7 = (s16[33,32,128]{2,1,0:T(8,128)(2,1)S(1)}, s16[33,32,128]{2,1,0:T(8,128)(2,1)S(1)}, u32[]{:S(2)}, u32[]{:S(2)}) collective-permute-start(s16[33,32,128]{2,1,0:T(8,128)(2,1)S(1)} %get-tuple-element.51), channel_id=1, source_target_pairs={{1,2},{2,1},{5,6},{6,5},{9,10},{10,9},{13,14},{14,13},{17,18},{18,... | collective-permute-start | bytes 811016 | tf_op jit(solution)/shard_map/ppermute | solution.py:397
  100.1 6.8 %collective-permute-start.8 = (s16[33,32,128]{2,1,0:T(8,128)(2,1)S(1)}, s16[33,32,128]{2,1,0:T(8,128)(2,1)S(1)}, u32[]{:S(2)}, u32[]{:S(2)}) collective-permute-start(s16[33,32,128]{2,1,0:T(8,128)(2,1)S(1)} %get-tuple-element.52), channel_id=1, source_target_pairs={{0,1},{1,0},{2,3},{3,2},{4,5},{5,4},{6,7},{7,6},{8,9},{9,8},{10,11... | collective-permute-start | bytes 811016 | tf_op jit(solution)/shard_map/ppermute | solution.py:391
  100.7 6.2 %collective-permute-start.9 = (s16[33,32,128]{2,1,0:T(8,128)(2,1)S(1)}, s16[33,32,128]{2,1,0:T(8,128)(2,1)S(1)}, u32[]{:S(2)}, u32[]{:S(2)}) collective-permute-start(s16[33,32,128]{2,1,0:T(8,128)(2,1)S(1)} %get-tuple-element.53), channel_id=1, source_target_pairs={{1,2},{2,1},{5,6},{6,5},{9,10},{10,9},{13,14},{14,13},{17,18},{18,... | collective-permute-start | bytes 811016 | tf_op jit(solution)/shard_map/ppermute | solution.py:397
  119.2 3.1 %collective-permute-start.10 = (s16[65,16,128]{2,1,0:T(8,128)(2,1)S(1)}, s16[65,16,128]{2,1,0:T(8,128)(2,1)S(1)}, u32[]{:S(2)}, u32[]{:S(2)}) collective-permute-start(s16[65,16,128]{2,1,0:T(8,128)(2,1)S(1)} %get-tuple-element.56), channel_id=1, source_target_pairs={{0,4},{4,0},{8,12},{12,8},{16,20},{20,16},{24,28},{28,24},{32,36},... | collective-permute-start | bytes 798728 | tf_op jit(solution)/shard_map/ppermute | solution.py:391
  119.3 9.8 %collective-permute-start.11 = (s16[65,16,128]{2,1,0:T(8,128)(2,1)S(1)}, s16[65,16,128]{2,1,0:T(8,128)(2,1)S(1)}, u32[]{:S(2)}, u32[]{:S(2)}) collective-permute-start(s16[65,16,128]{2,1,0:T(8,128)(2,1)S(1)} %get-tuple-element.57), channel_id=1, source_target_pairs={{4,8},{12,16},{20,24},{28,32},{36,40},{44,48},{52,56},{60,64},{68,... | collective-permute-start | bytes 798728 | tf_op jit(solution)/shard_map/ppermute | solution.py:397
  129.8 6.8 %collective-permute-start.12 = (s16[17,32,128]{2,1,0:T(8,128)(2,1)S(1)}, s16[17,32,128]{2,1,0:T(8,128)(2,1)S(1)}, u32[]{:S(2)}, u32[]{:S(2)}) collective-permute-start(s16[17,32,128]{2,1,0:T(8,128)(2,1)S(1)} %get-tuple-element.59), channel_id=1, source_target_pairs={{0,1},{1,0},{2,3},{3,2},{4,5},{5,4},{6,7},{7,6},{8,9},{9,8},{10,11... | collective-permute-start | bytes 417800 | tf_op jit(solution)/shard_map/ppermute | solution.py:391
  133.5 3.0 %collective-permute-start.13 = (s16[17,32,128]{2,1,0:T(8,128)(2,1)S(1)}, s16[17,32,128]{2,1,0:T(8,128)(2,1)S(1)}, u32[]{:S(2)}, u32[]{:S(2)}) collective-permute-start(s16[17,32,128]{2,1,0:T(8,128)(2,1)S(1)} %get-tuple-element.60), channel_id=1, source_target_pairs={{1,2},{2,1},{5,6},{6,5},{9,10},{10,9},{13,14},{14,13},{17,18},{18,... | collective-permute-start | bytes 417800 | tf_op jit(solution)/shard_map/ppermute | solution.py:397
  137.1 6.7 %collective-permute-start.14 = (s16[17,32,128]{2,1,0:T(8,128)(2,1)S(1)}, s16[17,32,128]{2,1,0:T(8,128)(2,1)S(1)}, u32[]{:S(2)}, u32[]{:S(2)}) collective-permute-start(s16[17,32,128]{2,1,0:T(8,128)(2,1)S(1)} %get-tuple-element.61.refs_0_), channel_id=1, source_target_pairs={{1,2},{3,0},{2,1},{0,3},{5,6},{7,4},{6,5},{4,7},{9,10},{11,8},{10,... | collective-permute-start | bytes 417800 | tf_op jit(solution)/shard_map/ppermute | solution.py:397
  138.8 8.4 %collective-permute-start.16 = (s16[17,32,128]{2,1,0:T(8,128)(2,1)S(1)}, s16[17,32,128]{2,1,0:T(8,128)(2,1)S(1)}, u32[]{:S(2)}, u32[]{:S(2)}) collective-permute-start(s16[17,32,128]{2,1,0:T(8,128)(2,1)S(1)} %get-tuple-element.62.refs_1_), channel_id=1, source_target_pairs={{0,1},{1,0},{2,3},{3,2},{4,5},{5,4},{6,7},{7,6},{8,9},{9,8},{10,11... | collective-permute-start | bytes 417800 | tf_op jit(solution)/shard_map/ppermute | solution.py:391
  142.1 6.7 %collective-permute-start.18 = (s16[17,32,128]{2,1,0:T(8,128)(2,1)S(1)}, s16[17,32,128]{2,1,0:T(8,128)(2,1)S(1)}, u32[]{:S(2)}, u32[]{:S(2)}) collective-permute-start(s16[17,32,128]{2,1,0:T(8,128)(2,1)S(1)} %get-tuple-element.61.refs_0_), channel_id=1, source_target_pairs={{0,1},{1,0},{2,3},{3,2},{4,5},{5,4},{6,7},{7,6},{8,9},{9,8},{10,11... | collective-permute-start | bytes 417800 | tf_op jit(solution)/shard_map/ppermute | solution.py:391
  142.1 7.2 %collective-permute-start.19 = (s16[17,32,128]{2,1,0:T(8,128)(2,1)S(1)}, s16[17,32,128]{2,1,0:T(8,128)(2,1)S(1)}, u32[]{:S(2)}, u32[]{:S(2)}) collective-permute-start(s16[17,32,128]{2,1,0:T(8,128)(2,1)S(1)} %get-tuple-element.62.refs_1_), channel_id=1, source_target_pairs={{1,2},{3,0},{2,1},{0,3},{5,6},{7,4},{6,5},{4,7},{9,10},{11,8},{10,... | collective-permute-start | bytes 417800 | tf_op jit(solution)/shard_map/ppermute | solution.py:397
  143.7 7.4 %collective-permute-start.15 = (s16[17,32,128]{2,1,0:T(8,128)(2,1)S(1)}, s16[17,32,128]{2,1,0:T(8,128)(2,1)S(1)}, u32[]{:S(2)}, u32[]{:S(2)}) collective-permute-start(s16[17,32,128]{2,1,0:T(8,128)(2,1)S(1)} %collective-permute-done.14.refs_4_), channel_id=1, source_target_pairs={{0,1},{1,0},{2,3},{3,2},{4,5},{5,4},{6,7},{7,6},{8,9},{9,8},{10,11... | collective-permute-start | bytes 417800 | tf_op jit(solution)/shard_map/ppermute | solution.py:391
  147.2 6.3 %collective-permute-start.17 = (s16[17,32,128]{2,1,0:T(8,128)(2,1)S(1)}, s16[17,32,128]{2,1,0:T(8,128)(2,1)S(1)}, u32[]{:S(2)}, u32[]{:S(2)}) collective-permute-start(s16[17,32,128]{2,1,0:T(8,128)(2,1)S(1)} %collective-permute-done.16.refs_3_), channel_id=1, source_target_pairs={{1,2},{3,0},{2,1},{0,3},{5,6},{7,4},{6,5},{4,7},{9,10},{11,8},{10,... | collective-permute-start | bytes 417800 | tf_op jit(solution)/shard_map/ppermute | solution.py:397
  (2 other events, 2.9 us)
